TPU v7x, 32 devices: a whole 2x2x4 slice. The times are simulated.
32 devices in a mesh: pipe: 2 (over x), dp: 4 (over y, core), expert: 4 (over z).
Axes of the slice: x: 2, y: 2, z: 4, core: 2. Of those that a mesh axis runs over, the one named last changes fastest.
Arguments:
- tokens: bfloat16 [512, 6144], P('expert', 'dp'), may hold values from -6 to 6
- expert_ids: int32 [512, 2], P('expert'), may hold values from 0 to 7, all different within a row; in each aligned block of 128 rows (0 to 127, 128 to 255, ...) at most 34 rows name the same one
- gates: float32 [512, 2], P('expert'), may hold values from 0.1 to 1
- w_up: bfloat16 [16, 6144, 4096], P('expert', 'dp', 'pipe'), may hold values from -0.078125 to 0.078125
- w_down: bfloat16 [16, 4096, 6144], P('expert', 'pipe', 'dp'), may hold values from -0.0625 to 0.0625
- cotangent: bfloat16 [512, 6144], P('expert', 'dp'), may hold values from -6 to 6
Outputs:
- output: bfloat16 [512, 6144], P('expert', ('dp', 'pipe'))
- token_grad: bfloat16 [512, 6144], P('expert', ('dp', 'pipe'))
- up_grad: bfloat16 [16, 6144, 4096], P('expert', 'dp', 'pipe')
- down_grad: bfloat16 [16, 4096, 6144], P('expert', 'pipe', 'dp')
Inputs may be any that keep to these rules, and one draw needn't show every extreme that they name: `expert_ids`: the two ids of a token differ. Among the 128 rows of one index of the expert axis (aligned blocks of rows), no expert is named by more than 34 rows, a bound that some block reaches.
All inputs are finite; a program needn't handle non-finite values.
Results may differ from a plain program's by a relative error of at most 0.027.
Values may be sent and summed in bfloat16 or wider, within the bound.
A program may use at most 192 MiB of HBM per device.

v0:
```python
import jax
import jax.numpy as jnp
from jax import lax
from jax.sharding import PartitionSpec as P

E = 8
TOP = 2
CAP = 34


def silu_slope(pre):
    sigma = jax.nn.sigmoid(pre)
    return sigma * (1.0 + pre * (1.0 - sigma))


def routing_tables(expert_ids, gates):
    count_rows = expert_ids.shape[0]
    chosen = expert_ids.reshape(-1)
    one_hot = (chosen[:, None] == jnp.arange(E, dtype=jnp.int32)[None, :]).astype(jnp.int32)
    earlier = jnp.cumsum(one_hot, axis=0) - one_hot
    position = jnp.sum(earlier * one_hot, axis=1)
    slot_index = (chosen * CAP + position).reshape(count_rows, TOP)
    columns = jnp.arange(E * CAP, dtype=jnp.int32)[None, :]
    routing = jnp.zeros((count_rows, E * CAP), jnp.float32)
    weighting = jnp.zeros((count_rows, E * CAP), jnp.float32)
    for which in range(TOP):
        matches = (slot_index[:, which][:, None] == columns).astype(jnp.float32)
        routing = routing + matches
        weighting = weighting + matches * gates[:, which][:, None]
    return (routing, weighting)


def to_pairs(per_expert, groups, pairs):
    doubled = jnp.repeat(per_expert.reshape(E, CAP, -1), 2, axis=0)
    return doubled.reshape(groups, pairs, CAP, per_expert.shape[-1])


def from_pairs(per_pair):
    summed = jnp.sum(per_pair.reshape(E, 2, CAP, per_pair.shape[-1]), axis=1)
    return summed.reshape(E * CAP, per_pair.shape[-1])


def on_device(tokens, expert_ids, gates, w_up, w_down, cotangent):
    groups = lax.axis_size("expert")
    pairs = w_up.shape[0]
    routing, weighting = routing_tables(expert_ids, gates)
    buffer = jnp.einsum(
        "ts,td->sd", routing.astype(jnp.bfloat16), tokens, preferred_element_type=jnp.float32
    ).astype(jnp.bfloat16)
    scaled = jnp.einsum(
        "ts,td->sd", weighting, cotangent.astype(jnp.float32), precision=lax.Precision.HIGHEST
    ).astype(jnp.bfloat16)
    arrived = lax.all_to_all(
        to_pairs(buffer, groups, pairs), "expert", split_axis=0, concat_axis=0, tiled=True
    )
    pre_part = jnp.einsum("spcd,pdh->spch", arrived, w_up, preferred_element_type=jnp.float32)
    pre_share = lax.psum_scatter(
        pre_part.astype(jnp.bfloat16), "dp", scatter_dimension=0, tiled=True
    ).astype(jnp.float32)
    hidden_share = jax.nn.silu(pre_share).astype(jnp.bfloat16)
    hidden = lax.all_gather(hidden_share, "dp", axis=0, tiled=True)
    partial_out = jnp.einsum("spch,phd->spcd", hidden, w_down, preferred_element_type=jnp.float32)
    reduced = lax.psum_scatter(
        partial_out.astype(jnp.bfloat16), "pipe", scatter_dimension=3, tiled=True
    ).astype(jnp.float32)
    returned = lax.all_to_all(
        reduced.astype(jnp.bfloat16), "expert", split_axis=0, concat_axis=0, tiled=True
    ).astype(reduced.dtype)
    expert_out = from_pairs(returned)
    output = jnp.dot(weighting, expert_out, precision=lax.Precision.HIGHEST).astype(jnp.bfloat16)
    grad_rows = lax.all_to_all(
        to_pairs(scaled, groups, pairs), "expert", split_axis=0, concat_axis=0, tiled=True
    )
    grad_part = jnp.einsum("spcd,phd->spch", grad_rows, w_down, preferred_element_type=jnp.float32)
    grad_share = lax.psum_scatter(
        grad_part.astype(jnp.bfloat16), "dp", scatter_dimension=0, tiled=True
    ).astype(jnp.float32)
    grad_pre_share = (grad_share * silu_slope(pre_share)).astype(jnp.bfloat16)
    grad_pre = lax.all_gather(grad_pre_share, "dp", axis=0, tiled=True)
    down_grad = jnp.einsum(
        "spch,spcd->phd", hidden, grad_rows, preferred_element_type=jnp.float32
    ).astype(jnp.bfloat16)
    up_grad = jnp.einsum(
        "spcd,spch->pdh", arrived, grad_pre, preferred_element_type=jnp.float32
    ).astype(jnp.bfloat16)
    back_part = jnp.einsum("spch,pdh->spcd", grad_pre, w_up, preferred_element_type=jnp.float32)
    back_sum = lax.psum_scatter(
        back_part.astype(jnp.bfloat16), "pipe", scatter_dimension=3, tiled=True
    ).astype(jnp.float32)
    back_home = lax.all_to_all(
        back_sum.astype(jnp.bfloat16), "expert", split_axis=0, concat_axis=0, tiled=True
    ).astype(back_sum.dtype)
    back_expert = from_pairs(back_home)
    token_grad = jnp.dot(routing, back_expert, precision=lax.Precision.HIGHEST).astype(jnp.bfloat16)
    return (output, token_grad, up_grad, down_grad)


def solution(mesh):
    return jax.shard_map(
        on_device,
        mesh=mesh,
        in_specs=(
            P("expert", "dp"),
            P("expert", None),
            P("expert", None),
            P("expert", "dp", "pipe"),
            P("expert", "pipe", "dp"),
            P("expert", "dp"),
        ),
        out_specs=(
            P("expert", ("dp", "pipe")),
            P("expert", ("dp", "pipe")),
            P("expert", "dp", "pipe"),
            P("expert", "pipe", "dp"),
        ),
        check_vma=False,
    )
```

profile of v0, /device:TPU:0, one launch (start us, length us, event | category | flops | bytes accessed | tf_op | source)
XLA Modules:
  0.0 382.5 jit_solution(12173975438261444801)
XLA Ops:
  14.3 3.2 copy.56
  17.5 6.5 %all-to-all-start = ((bf16[4,4,34,1536]{3,1,2,0:T(4,128)(2,1)}), bf16[4,4,34,1536]{3,1,2,0:T(4,128)(2,1)S(1)}, u32[]{:S(2)}, u32[]{:S(2)}) async-start(bf16[4,4,34,1536]{3,1,2,0:T(4,128)(2,1)} %copy.56), calls=%async_computation | async-start | bytes 3342336 | tf_op jit(solution)/shard_map/all_to_all | solution.py:53
  27.4 2.7 broadcast_in_dim.9
  30.2 5.0 %reshape_reshape.7 = bf16[4,4,34,1536]{3,1,0,2:T(4,128)(2,1)} reshape(bf16[8,2,34,1536]{3,1,0,2:T(2,128)(2,1)} %broadcast_in_dim.9) | data formatting | bytes 3342336 | tf_op jit(solution)/shard_map/reshape;reshape | solution.py:35
  35.1 3.2 copy.64
  38.3 24.6 %all-to-all-done = bf16[4,4,34,1536]{3,1,2,0:T(4,128)(2,1)S(1)} async-done(((bf16[4,4,34,1536]{3,1,2,0:T(4,128)(2,1)}), bf16[4,4,34,1536]{3,1,2,0:T(4,128)(2,1)S(1)}, u32[]{:S(2)}, u32[]{:S(2)}) %all-to-all-start) | async-done | bytes 1671200 | tf_op jit(solution)/shard_map/all_to_all | solution.py:53
  63.0 4.3 %all-to-all-start.2 = ((bf16[4,4,34,1536]{3,1,2,0:T(4,128)(2,1)}), bf16[4,4,34,1536]{3,1,2,0:T(4,128)(2,1)}, u32[]{:S(2)}, u32[]{:S(2)}) async-start(bf16[4,4,34,1536]{3,1,2,0:T(4,128)(2,1)} %copy.64), calls=%async_computation.3 | async-start | bytes 3342336 | tf_op jit(solution)/shard_map/all_to_all | solution.py:71
  67.6 12.6 %fusion.23 = bf16[4,4,34,2048]{3,2,0,1:T(8,128)(2,1)S(1)} fusion(bf16[4,1536,2048]{2,1,0:T(8,128)(2,1)} %param.9, bf16[4,4,34,1536]{3,1,2,0:T(4,128)(2,1)S(1)} %all-to-all-done), kind=kOutput, calls=%fused_computation.15 | convolution fusion | flops 3423666176 | bytes 29065216 | tf_op jit(solution)/shard_map/spcd,pdh->spch/dot_general | solution.py:56
  80.1 3.1 copy.58
  83.2 22.7 %all-to-all-done.2 = bf16[4,4,34,1536]{3,1,2,0:T(4,128)(2,1)} async-done(((bf16[4,4,34,1536]{3,1,2,0:T(4,128)(2,1)}), bf16[4,4,34,1536]{3,1,2,0:T(4,128)(2,1)}, u32[]{:S(2)}, u32[]{:S(2)}) %all-to-all-start.2) | async-done | bytes 1671200 | tf_op jit(solution)/shard_map/all_to_all | solution.py:71
  106.0 13.8 %fusion.26 = bf16[4,4,34,2048]{3,2,0,1:T(8,128)(2,1)S(1)} fusion(bf16[4,2048,1536]{2,1,0:T(8,128)(2,1)} %param.10, bf16[4,4,34,1536]{3,1,2,0:T(4,128)(2,1)} %all-to-all-done.2), kind=kOutput, calls=%fused_computation.16 | convolution fusion | flops 3423666176 | bytes 29065216 | tf_op jit(solution)/shard_map/spcd,phd->spch/dot_general | solution.py:74
  119.8 3.1 copy.66
  124.1 88.0 %all-reduce.5.cloned.1.call-done = (bf16[4,4,34,2048]{3,1,2,0:T(4,128)(2,1)}, bf16[4,4,34,2048]{3,1,2,0:T(4,128)(2,1)}) async-done(((bf16[4,4,34,2048]{3,1,2,0:T(4,128)(2,1)}, bf16[4,4,34,2048]{3,1,2,0:T(4,128)(2,1)}), (bf16[4,4,34,2048]{3,1,2,0:T(4,128)(2,1)}, bf16[4,4,34,2048]{3,1,2,0:T(4,128)(2,1)})) %all-reduce.5.cloned.1.call-update) | async-done | bytes 4456464
  212.1 2.4 constant_dynamic-slice_fusion
  214.5 1.9 fusion.43
  217.2 25.1 %all-gather.3.cloned.1.call-done = bf16[4,4,34,2048]{3,2,0,1:T(8,128)(2,1)} async-done(((bf16[1,4,34,2048]{3,2,0,1:T(8,128)(2,1)}), bf16[4,4,34,2048]{3,2,0,1:T(8,128)(2,1)}) %all-gather.3.cloned.1.call-update) | async-done | bytes 2228240 | tf_op jit(solution)/shard_map/all_gather | solution.py:61
  242.3 14.7 %fusion.29 = bf16[4,4,34,1536]{3,2,0,1:T(8,128)(2,1)} fusion(bf16[4,4,34,2048]{3,2,0,1:T(8,128)(2,1)} %all-gather.3.cloned.1.call-done, bf16[4,2048,1536]{2,1,0:T(8,128)(2,1)} %param.10), kind=kOutput, calls=%fused_computation.17 | convolution fusion | flops 3423387648 | bytes 29065216 | tf_op jit(solution)/shard_map/spch,phd->spcd/dot_general | solution.py:62
  257.1 12.9 %all-gather.5.cloned.1.call-done = bf16[4,4,34,2048]{3,2,0,1:T(8,128)(2,1)} async-done(((bf16[1,4,34,2048]{3,2,0,1:T(8,128)(2,1)}), bf16[4,4,34,2048]{3,2,0,1:T(8,128)(2,1)}) %all-gather.5.cloned.1.call-update) | async-done | bytes 2228240 | tf_op jit(solution)/shard_map/all_gather | solution.py:79
  270.0 14.8 %fusion.20 = bf16[4,4,34,1536]{3,2,0,1:T(8,128)(2,1)} fusion(bf16[4,4,34,2048]{3,2,0,1:T(8,128)(2,1)} %all-gather.5.cloned.1.call-done, bf16[4,1536,2048]{2,1,0:T(8,128)(2,1)} %param.9), kind=kOutput, calls=%fused_computation.14 | convolution fusion | flops 3423387648 | bytes 29065216 | tf_op jit(solution)/shard_map/spch,pdh->spcd/dot_general | solution.py:86
  284.8 18.3 %reduce-scatter.3.cloned.1.call-done = bf16[4,4,34,768]{3,2,0,1:T(8,128)(2,1)} async-done(((bf16[4,4,34,1536]{3,2,0,1:T(8,128)(2,1)}), bf16[4,4,34,768]{3,2,0,1:T(8,128)(2,1)}) %reduce-scatter.3.cloned.1.call-update) | async-done | bytes 835600 | tf_op jit(solution)/shard_map/reduce_scatter | solution.py:63
  303.1 2.7 copy.60
  305.8 4.6 %all-to-all-start.1 = ((bf16[4,4,34,768]{3,1,2,0:T(4,128)(2,1)}), bf16[4,4,34,768]{3,1,2,0:T(4,128)(2,1)S(1)}, u32[]{:S(2)}, u32[]{:S(2)}) async-start(bf16[4,4,34,768]{3,1,2,0:T(4,128)(2,1)} %copy.60), calls=%async_computation.2 | async-start | bytes 1671168 | tf_op jit(solution)/shard_map/all_to_all | solution.py:66
  310.4 14.8 %bitcast_convert_fusion.1 = bf16[4,1536,2048]{2,1,0:T(8,128)(2,1)} fusion(bf16[4,4,34,2048]{3,2,0,1:T(8,128)(2,1)} %all-gather.5.cloned.1.call-done, bf16[4,4,34,1536]{3,1,2,0:T(4,128)(2,1)S(1)} %copy-done.3), kind=kOutput, calls=%fused_computation.1 | convolution fusion | flops 3435134976 | bytes 29065216 | tf_op jit(solution)/shard_map/spcd,spch->pdh/dot_general | solution.py:83
  325.2 10.5 %reduce-scatter.5.cloned.1.call-done = bf16[4,4,34,768]{3,2,0,1:T(8,128)(2,1)} async-done(((bf16[4,4,34,1536]{3,2,0,1:T(8,128)(2,1)}), bf16[4,4,34,768]{3,2,0,1:T(8,128)(2,1)}) %reduce-scatter.5.cloned.1.call-update) | async-done | bytes 835600 | tf_op jit(solution)/shard_map/reduce_scatter | solution.py:87
  335.7 2.8 copy.68
  338.5 5.0 %all-to-all-start.3 = ((bf16[4,4,34,768]{3,1,2,0:T(4,128)(2,1)}), bf16[4,4,34,768]{3,1,2,0:T(4,128)(2,1)}, u32[]{:S(2)}, u32[]{:S(2)}) async-start(bf16[4,4,34,768]{3,1,2,0:T(4,128)(2,1)} %copy.68), calls=%async_computation.5 | async-start | bytes 1671168 | tf_op jit(solution)/shard_map/all_to_all | solution.py:90
  343.5 14.4 %bitcast_convert_fusion = bf16[4,2048,1536]{2,1,0:T(8,128)(2,1)} fusion(bf16[4,4,34,2048]{3,2,0,1:T(8,128)(2,1)} %all-gather.3.cloned.1.call-done, bf16[4,4,34,1536]{3,1,2,0:T(4,128)(2,1)} %all-to-all-done.2), kind=kOutput, calls=%fused_computation | convolution fusion | flops 3435134976 | bytes 29065216 | tf_op jit(solution)/shard_map/spch,spcd->phd/dot_general | solution.py:80
  358.4 2.5 reshape.62
  360.9 3.4 reduce_sum.31
  366.2 2.8 copy.69
  369.1 2.7 reshape.64
  371.8 2.0 reduce_sum.32
  (56 shorter events, 17.1 us)
Async XLA Ops:
  7.2 3.0 copy-start
  17.4 6.5 %copy-start.5 = (f32[128,2]{0,1:T(2,128)S(1)}, f32[128,2]{0,1:T(2,128)}, u32[]{:S(2)}) copy-start(f32[128,2]{0,1:T(2,128)} %param.8) | copy-start | bytes 3076
  17.4 6.5 %copy-start.4 = (bf16[128,1536]{1,0:T(8,128)(2,1)S(1)}, bf16[128,1536]{1,0:T(8,128)(2,1)}, u32[]{:S(2)}) copy-start(bf16[128,1536]{1,0:T(8,128)(2,1)} %param.11) | copy-start | bytes 1179652
  17.5 45.5 %all-to-all-start = ((bf16[4,4,34,1536]{3,1,2,0:T(4,128)(2,1)}), bf16[4,4,34,1536]{3,1,2,0:T(4,128)(2,1)S(1)}, u32[]{:S(2)}, u32[]{:S(2)}) async-start(bf16[4,4,34,1536]{3,1,2,0:T(4,128)(2,1)} %copy.56), calls=%async_computation | async-start | bytes 3342336 | tf_op jit(solution)/shard_map/all_to_all | solution.py:53
  63.0 17.2 %copy-start.2 = (bf16[4,4,34,1536]{3,1,2,0:T(4,128)(2,1)}, bf16[4,4,34,1536]{3,1,2,0:T(4,128)(2,1)S(1)}, u32[]{:S(2)}) copy-start(bf16[4,4,34,1536]{3,1,2,0:T(4,128)(2,1)S(1)} %all-to-all-done) | copy-start | bytes 5013508
  63.0 43.0 %all-to-all-start.2 = ((bf16[4,4,34,1536]{3,1,2,0:T(4,128)(2,1)}), bf16[4,4,34,1536]{3,1,2,0:T(4,128)(2,1)}, u32[]{:S(2)}, u32[]{:S(2)}) async-start(bf16[4,4,34,1536]{3,1,2,0:T(4,128)(2,1)} %copy.64), calls=%async_computation.3 | async-start | bytes 3342336 | tf_op jit(solution)/shard_map/all_to_all | solution.py:71
  67.3 144.8 %all-reduce.5.cloned.1.call-start = ((), (), s32[]{:S(2)}) async-start(), calls=%async_computation.10 | async-start | bytes 8912896
  122.9 0.7 copy-start.6
  122.9 119.4 %all-gather.3.cloned.1.call-start = ((), (), s32[]{:S(2)}) async-start(), calls=%async_computation.6 | async-start | bytes 3276800 | tf_op jit(solution)/shard_map/all_gather | solution.py:61
  216.4 53.6 %all-gather.5.cloned.1.call-start = ((), (), s32[]{:S(2)}) async-start(), calls=%async_computation.8 | async-start | bytes 3276800 | tf_op jit(solution)/shard_map/all_gather | solution.py:79
  217.1 85.9 %reduce-scatter.3.cloned.1.call-start = ((), (), s32[]{:S(2)}) async-start(), calls=%async_computation.7 | async-start | bytes 2949120 | tf_op jit(solution)/shard_map/reduce_scatter | solution.py:63
  257.0 78.7 %reduce-scatter.5.cloned.1.call-start = ((), (), s32[]{:S(2)}) async-start(), calls=%async_computation.9 | async-start | bytes 2949120 | tf_op jit(solution)/shard_map/reduce_scatter | solution.py:87
  284.8 25.6 %copy-start.3 = (bf16[4,4,34,1536]{3,1,2,0:T(4,128)(2,1)S(1)}, bf16[4,4,34,1536]{3,1,2,0:T(4,128)(2,1)}, u32[]{:S(2)}) copy-start(bf16[4,4,34,1536]{3,1,2,0:T(4,128)(2,1)} %copy-done.2) | copy-start | bytes 5013508
  305.8 32.7 %all-to-all-start.1 = ((bf16[4,4,34,768]{3,1,2,0:T(4,128)(2,1)}), bf16[4,4,34,768]{3,1,2,0:T(4,128)(2,1)S(1)}, u32[]{:S(2)}, u32[]{:S(2)}) async-start(bf16[4,4,34,768]{3,1,2,0:T(4,128)(2,1)} %copy.60), calls=%async_computation.2 | async-start | bytes 1671168 | tf_op jit(solution)/shard_map/all_to_all | solution.py:66
  338.5 27.7 %all-to-all-start.3 = ((bf16[4,4,34,768]{3,1,2,0:T(4,128)(2,1)}), bf16[4,4,34,768]{3,1,2,0:T(4,128)(2,1)}, u32[]{:S(2)}, u32[]{:S(2)}) async-start(bf16[4,4,34,768]{3,1,2,0:T(4,128)(2,1)} %copy.68), calls=%async_computation.5 | async-start | bytes 1671168 | tf_op jit(solution)/shard_map/all_to_all | solution.py:90
  371.8 4.0 %copy-start.1 = (bf16[128,1536]{1,0:T(8,128)(2,1)S(1)}, bf16[128,1536]{1,0:T(8,128)(2,1)}, u32[]{:S(2)}) copy-start(bf16[128,1536]{1,0:T(8,128)(2,1)} %param.6) | copy-start | bytes 1179652
Sparse Core Ops, SparseCore 0:
  123.0 89.0 all-reduce.4
  216.5 25.6 all-gather.2
  244.4 25.5 all-gather.4
  272.7 30.3 reduce-scatter.2
  305.3 30.3 reduce-scatter.4
where the time goes:
time: 389 us; the launch traced here: 382 us
  waiting for transfers between devices  203 us (52%)
  matrix products  90.5 us (23%)
  local copies, waits for them, and re-layouts  45.2 us (12%)
  starting transfers between devices  21 us (5%)
  between operations  14.2 us (4%)
  other arithmetic  8.78 us (2%)
    unnamed x6, waiting for transfers between devices  88.8 us
    all_gather x1, waiting for transfers between devices, on_device(): hidden = lax.all_gather(hidden_share, 'dp', axis=0, tiled=True)  25.1 us
    all_to_all x1, waiting for transfers between devices, on_device(): lax.all_to_all(to_pairs(buffer, groups, pairs), 'expert', split_axis=0, c...  24.6 us
    all_to_all x1, waiting for transfers between devices, on_device(): lax.all_to_all(to_pairs(scaled, groups, pairs), 'expert', split_axis=0, c...  22.7 us
    reduce_scatter x1, waiting for transfers between devices, on_device(): lax.psum_scatter(partial_out.astype(jnp.bfloat16), 'pipe', scatter_dimens...  18.3 us
    dot_general x1, matrix products, on_device(): jnp.einsum('spch,pdh->spcd', grad_pre, w_up, preferred_element_type=jnp.f...  14.8 us
    dot_general x1, matrix products, on_device(): jnp.einsum('spcd,spch->pdh', arrived, grad_pre, preferred_element_type=jn...  14.8 us
    dot_general x1, matrix products, on_device(): jnp.einsum('spch,phd->spcd', hidden, w_down, preferred_element_type=jnp.f...  14.7 us
  transfers between devices with their start and end apart: 9, of which 7 were waited for; matrix products, arithmetic and copies ran while one was open for 27% of the time, Pallas kernels for 0%

commit v1 on v0

v1 whole, which is shorter than its diff:
```python
import jax
import jax.numpy as jnp
from jax import lax
from jax.sharding import PartitionSpec as P

CAP = 34
BF = jnp.bfloat16
F32 = jnp.float32


def silu_slope(pre):
    sigma = jax.nn.sigmoid(pre)
    return sigma * (1.0 + pre * (1.0 - sigma))


def swap(value, axis, bit):
    count = lax.axis_size(axis)
    return lax.ppermute(value, axis, [(i, i ^ bit) for i in range(count)])


def pick(value, index, axis):
    return lax.dynamic_index_in_dim(value, index, axis, keepdims=False)


def sum_over_features(part):
    count = lax.axis_size("dp")
    pairs, rows, hidden = part.shape
    if count != 4 or pairs % 4:
        return lax.psum_scatter(part, "dp", scatter_dimension=2, tiled=True).astype(F32)
    me = lax.axis_index("dp")
    core, chip = me % 2, me // 2
    cut = part.reshape(2, 2, pairs // 4, rows, hidden)
    other = swap(pick(cut, 1 - core, 1), "dp", 1)
    near = (pick(cut, core, 1).astype(F32) + other.astype(F32)).astype(BF)
    far = swap(pick(near, 1 - chip, 0), "dp", 2)
    return pick(near, chip, 0).astype(F32) + far.astype(F32)


def share_of_features(value, pairs):
    if lax.axis_size("dp") != 4 or pairs % 4:
        return lax.all_gather(value, "dp", axis=2, tiled=True)
    return lax.all_gather(value, "dp", axis=0, tiled=True)


def sum_over_hidden(part):
    count = lax.axis_size("pipe")
    part = part.astype(BF)
    if count != 2:
        return lax.psum_scatter(part, "pipe", scatter_dimension=2, tiled=True).astype(F32)
    me = lax.axis_index("pipe")
    width = part.shape[2] // 2
    sent = swap(lax.dynamic_slice_in_dim(part, (1 - me) * width, width, 2), "pipe", 1)
    return lax.dynamic_slice_in_dim(part, me * width, width, 2).astype(F32) + sent.astype(F32)


def on_device(tokens, expert_ids, gates, w_up, w_down, cotangent):
    groups = lax.axis_size("expert")
    pairs, features, hidden_width = w_up.shape
    halves = 2 if pairs % 2 == 0 else 1
    sets = pairs // halves
    rows = groups * CAP
    own = tokens.shape[0]
    count = groups * own

    meta = jnp.concatenate([expert_ids.astype(F32).T, gates.T], axis=0)
    meta = lax.all_gather(meta, "expert", axis=1, tiled=True)
    all_tokens = lax.all_gather(tokens, "expert", axis=0, tiled=True)
    all_cotangent = lax.all_gather(cotangent, "expert", axis=0, tiled=True)

    pair_ids = lax.axis_index("expert") * pairs + jnp.arange(pairs, dtype=jnp.int32)
    wanted = (pair_ids // 2).astype(F32)[:, None]
    first, second = meta[0:1] == wanted, meta[1:2] == wanted
    chosen = first | second
    weight = jnp.where(first, meta[2:3], 0.0) + jnp.where(second, meta[3:4], 0.0)
    before = jnp.arange(count)[:, None] < jnp.arange(count)[None, :]
    position = jnp.dot(chosen.astype(BF), before.astype(BF), preferred_element_type=F32)
    position = jnp.where(chosen, position, -1.0)
    slots = jnp.arange(rows, dtype=jnp.int32).astype(F32)[None, :, None]
    match = position[:, None, :] == slots
    routing = match.astype(BF).reshape(pairs * rows, count)
    row_weight = jnp.sum(jnp.where(match, weight[:, None, :], 0.0), axis=2)
    set_routing = match[::halves].astype(BF).reshape(sets * rows, count)
    set_weight = row_weight[::halves]

    arrived = jnp.dot(routing, all_tokens, preferred_element_type=F32)
    arrived = arrived.astype(BF).reshape(pairs, rows, features)
    pre_part = jnp.einsum("pcd,pdh->pch", arrived, w_up, preferred_element_type=F32).astype(BF)
    pre_share = sum_over_features(pre_part)

    grad_rows = jnp.dot(routing, all_cotangent, preferred_element_type=F32)
    grad_rows = (grad_rows.reshape(pairs, rows, features) * row_weight[:, :, None]).astype(BF)
    grad_part = jnp.einsum("pcd,phd->pch", grad_rows, w_down, preferred_element_type=F32).astype(BF)

    hidden = share_of_features(jax.nn.silu(pre_share).astype(BF), pairs)
    grad_share = sum_over_features(grad_part)
    grad_pre = share_of_features((grad_share * silu_slope(pre_share)).astype(BF), pairs)

    def by_set(value):
        return value.reshape((sets, halves) + value.shape[1:])

    out_part = jnp.einsum("rhck,rhkd->rcd", by_set(hidden), by_set(w_down), preferred_element_type=F32)
    out_rows = sum_over_hidden(out_part)
    back_part = jnp.einsum("rhck,rhdk->rcd", by_set(grad_pre), by_set(w_up), preferred_element_type=F32)
    back_rows = sum_over_hidden(back_part)

    def home(value):
        flat = value.astype(BF).reshape(sets * rows, value.shape[2])
        placed = lax.dot_general(
            set_routing, flat, (((0,), (0,)), ((), ())), preferred_element_type=F32
        )
        return lax.psum_scatter(placed.astype(BF), "expert", scatter_dimension=0, tiled=True)

    output = home(out_rows * set_weight[:, :, None])
    token_grad = home(back_rows)
    down_grad = jnp.einsum("pch,pcd->phd", hidden, grad_rows, preferred_element_type=F32).astype(BF)
    up_grad = jnp.einsum("pcd,pch->pdh", arrived, grad_pre, preferred_element_type=F32).astype(BF)
    return (output, token_grad, up_grad, down_grad)


def solution(mesh):
    return jax.shard_map(
        on_device,
        mesh=mesh,
        in_specs=(
            P("expert", "dp"),
            P("expert", None),
            P("expert", None),
            P("expert", "dp", "pipe"),
            P("expert", "pipe", "dp"),
            P("expert", "dp"),
        ),
        out_specs=(
            P("expert", ("dp", "pipe")),
            P("expert", ("dp", "pipe")),
            P("expert", "dp", "pipe"),
            P("expert", "pipe", "dp"),
        ),
        check_vma=False,
    )
```

time: 389 us -> 260 us (0.67); the launches traced: 382 us -> 259 us
  waiting for transfers between devices: 203 us -> 118 us
  local copies, waits for them, and re-layouts: 45.2 us -> 6.12 us
  starting transfers between devices: 21 us -> 5.64 us
  blocking collectives: 0 us -> 13.5 us
    unnamed x6, waiting for transfers between devices: 88.8 us -> 1.95 us
    all_to_all x4 -> x0, waiting for transfers between devices: 47.4 us -> none  [the longest x1 24.6 us: on_device(): lax.all_to_all(to_pairs(buffer, groups, pairs), 'expert', split_axis=0, c...]
    all_gather x2 -> x4, waiting for transfers between devices: 38 us -> 76.3 us  [the longest x2 29.4 us: share_of_features(): return lax.all_gather(value, 'dp', axis=0, tiled=True)]
    ppermute x0 -> x6, waiting for transfers between devices: none -> 22.6 us  [swap(): return lax.ppermute(value, axis, [(i, i ^ bit) for i in range(count)])]
    all_to_all x4 -> x0, starting transfers between devices: 20.4 us -> none  [the longest x1 6.45 us: on_device(): lax.all_to_all(to_pairs(buffer, groups, pairs), 'expert', split_axis=0, c...]
    all_gather x0 -> x1, blocking collectives: none -> 13.5 us  [on_device(): meta = lax.all_gather(meta, 'expert', axis=1, tiled=True)]
    another operation x5 -> x0, local copies, waits for them, and re-layouts: 12.9 us -> none  [the longest x4 12.9 us: to_pairs(): return doubled.reshape(groups, pairs, CAP, per_expert.shape[-1])]
    reduce_scatter x2, waiting for transfers between devices: 28.7 us -> 16.8 us  [home(): lax.psum_scatter(placed.astype(BF), 'expert', scatter_dimension=0, tiled=...]
  transfers between devices with their start and end apart: 9 -> 12, of which waited for: 7 -> 7; matrix products, arithmetic and copies ran while one was open for 27% -> 41% of each run, Pallas kernels for 0% -> 0%
where the time goes in v1:
time: 260 us; the launch traced here: 259 us
  waiting for transfers between devices  118 us (45%)
  matrix products  93.9 us (36%)
  between operations  14.3 us (6%)
  blocking collectives  13.5 us (5%)
  other arithmetic  8.05 us (3%)
  local copies, waits for them, and re-layouts  6.12 us (2%)
  starting transfers between devices  5.64 us (2%)
    all_gather x2, waiting for transfers between devices, share_of_features(): return lax.all_gather(value, 'dp', axis=0, tiled=True)  29.4 us
    all_gather x1, waiting for transfers between devices, on_device(): all_tokens = lax.all_gather(tokens, 'expert', axis=0, tiled=True)  24.8 us
    ppermute x6, waiting for transfers between devices, swap(): return lax.ppermute(value, axis, [(i, i ^ bit) for i in range(count)])  22.6 us
    all_gather x1, waiting for transfers between devices, on_device(): all_cotangent = lax.all_gather(cotangent, 'expert', axis=0, tiled=True)  22.1 us
    reduce_scatter x2, waiting for transfers between devices, home(): lax.psum_scatter(placed.astype(BF), 'expert', scatter_dimension=0, tiled=...  16.8 us
    dot_general x1, matrix products, on_device(): jnp.einsum('pcd,phd->pch', grad_rows, w_down, preferred_element_type=F32)  14.6 us
    dot_general x1, matrix products, on_device(): jnp.einsum('pcd,pch->pdh', arrived, grad_pre, preferred_element_type=F32)  14.1 us
    dot_general x1, matrix products, on_device(): jnp.einsum('pch,pcd->phd', hidden, grad_rows, preferred_element_type=F32)  13.9 us
  transfers between devices with their start and end apart: 12, of which 7 were waited for; matrix products, arithmetic and copies ran while one was open for 41% of the time, Pallas kernels for 0%

profile of v1, /device:TPU:0, one launch (start us, length us, event | category | flops | bytes accessed | tf_op | source)
XLA Modules:
  0.0 259.3 jit_solution(3617907175519392589)
XLA Ops:
  7.9 0.7 all-gather.9.cloned.1.call-update
  9.5 0.7 pad_maximum_fusion
  10.2 13.5 %all_gather.15 = f32[4,512]{1,0:T(4,128)S(1)} all-gather(f32[4,128]{1,0:T(4,128)S(1)} %pad_maximum_fusion), channel_id=1, replica_groups=mesh['pipe'=2,'dp'=4,'expert'=4] {'expert'}, dimensions={1}, use_global_device_ids=true | all-gather | bytes 10240 | tf_op jit(solution)/shard_map/all_gather | solution.py:66
  24.6 24.8 %all-gather.5.cloned.1.call-done = bf16[512,1536]{1,0:T(8,128)(2,1)} async-done(((bf16[128,1536]{1,0:T(8,128)(2,1)}), bf16[512,1536]{1,0:T(8,128)(2,1)}) %all-gather.5.cloned.1.call-update) | async-done | bytes 1572880 | tf_op jit(solution)/shard_map/all_gather | solution.py:67
  49.4 2.4 convolution_convert_fusion.4
  51.8 12.8 %convolution_convert_fusion.3 = bf16[4,136,2048]{2,1,0:T(8,128)(2,1)S(1)} fusion(bf16[4,136,1536]{2,1,0:T(8,128)(2,1)S(1)} %bitcast.76, bf16[4,1536,2048]{2,1,0:T(8,128)(2,1)} %param.9), kind=kOutput, calls=%fused_computation.5 | convolution fusion | flops 3423666176 | bytes 29065216 | tf_op jit(solution)/shard_map/pcd,pdh->pch/dot_general | solution.py:87
  64.9 22.1 %all-gather.9.cloned.1.call-done = bf16[512,1536]{1,0:T(8,128)(2,1)} async-done(((bf16[128,1536]{1,0:T(8,128)(2,1)}), bf16[512,1536]{1,0:T(8,128)(2,1)}) %all-gather.9.cloned.1.call-update) | async-done | bytes 1572880 | tf_op jit(solution)/shard_map/all_gather | solution.py:68
  87.0 3.7 %fusion = bf16[4,136,1536]{2,1,0:T(8,128)(2,1)} fusion(f32[4,136]{1,0:T(4,128)S(1)} %select_reduce_fusion, bf16[512,1536]{1,0:T(8,128)(2,1)} %all-gather.9.cloned.1.call-done, f32[4,512]{1,0:T(4,128)S(1)} %convolution_select_fusion, f32[136]{0:T(256)S(1)} %iota_convert_fusion), kind=kOutput, calls=%fused_computation.3 | convolution fusion | flops 857587712 | bytes 3254944 | tf_op jit(solution)/shard_map/dot_general | solution.py:90
  90.7 14.6 %convolution_convert_fusion.2 = bf16[4,136,2048]{2,1,0:T(8,128)(2,1)} fusion(bf16[4,136,1536]{2,1,0:T(8,128)(2,1)} %fusion, bf16[4,2048,1536]{2,1,0:T(8,128)(2,1)} %param.10), kind=kOutput, calls=%fused_computation.4 | convolution fusion | flops 3423666176 | bytes 29065216 | tf_op jit(solution)/shard_map/pcd,phd->pch/dot_general | solution.py:92
  105.2 2.4 dynamic-slice_bitcast_fusion
  107.6 1.8 fusion.4
  109.5 0.9 dynamic-slice_bitcast_fusion.3
  110.3 1.5 collective-permute-start.1
  111.8 1.7 fusion.3
  113.5 0.9 dynamic-slice_bitcast_fusion.2
  114.9 11.1 %collective-permute-done.1 = bf16[1,136,2048]{2,1,0:T(8,128)(2,1)S(1)} collective-permute-done((bf16[1,136,2048]{2,1,0:T(8,128)(2,1)}, bf16[1,136,2048]{2,1,0:T(8,128)(2,1)S(1)}, u32[]{:S(2)}, u32[]{:S(2)}) %collective-permute-start.1) | collective-permute-done | bytes 557088 | tf_op jit(solution)/shard_map/ppermute | solution.py:18
  126.0 11.5 %collective-permute-done.4 = bf16[1,136,2048]{2,1,0:T(8,128)(2,1)S(1)} collective-permute-done((bf16[1,136,2048]{2,1,0:T(8,128)(2,1)}, bf16[1,136,2048]{2,1,0:T(8,128)(2,1)S(1)}, u32[]{:S(2)}, u32[]{:S(2)}) %collective-permute-start.4) | collective-permute-done | bytes 557088 | tf_op jit(solution)/shard_map/ppermute | solution.py:18
  137.5 1.6 fusion.7
  140.0 0.9 broadcast_compare_fusion
  141.0 20.6 %all-gather.7.cloned.1.call-done = bf16[4,136,2048]{2,1,0:T(8,128)(2,1)} async-done(((bf16[1,136,2048]{2,1,0:T(8,128)(2,1)}), bf16[4,136,2048]{2,1,0:T(8,128)(2,1)}) %all-gather.7.cloned.1.call-update) | async-done | bytes 2228240 | tf_op jit(solution)/shard_map/all_gather | solution.py:42
  161.5 12.8 %fusion.1 = bf16[2,136,1536]{2,1,0:T(8,128)(2,1)S(1)} fusion(bf16[2,2,136,2048]{3,2,1,0:T(8,128)(2,1)} %bitcast.79, bf16[2,2,2048,1536]{3,2,1,0:T(8,128)(2,1)} %bitcast.72), kind=kOutput, calls=%fused_computation.9 | convolution fusion | flops 3422969856 | bytes 28229632 | tf_op jit(solution)/shard_map/rhck,rhkd->rcd/dot_general | solution.py:101
  174.4 0.9 copy-done.4
  175.3 0.8 constant_dynamic-slice_fusion.1
  176.1 1.4 collective-permute-start.2
  177.5 8.8 %all-gather.11.cloned.1.call-done = bf16[4,136,2048]{2,1,0:T(8,128)(2,1)} async-done(((bf16[1,136,2048]{2,1,0:T(8,128)(2,1)}), bf16[4,136,2048]{2,1,0:T(8,128)(2,1)}) %all-gather.11.cloned.1.call-update) | async-done | bytes 2228240 | tf_op jit(solution)/shard_map/all_gather | solution.py:42
  186.3 13.9 %fusion.2 = bf16[2,136,1536]{2,1,0:T(8,128)(2,1)S(1)} fusion(bf16[2,2,136,2048]{3,2,1,0:T(8,128)(2,1)} %bitcast.78, bf16[2,2,1536,2048]{3,2,1,0:T(8,128)(2,1)} %bitcast.73), kind=kOutput, calls=%fused_computation.10 | convolution fusion | flops 3422969856 | bytes 28229632 | tf_op jit(solution)/shard_map/rhck,rhdk->rcd/dot_general | solution.py:103
  200.2 1.5 collective-permute-start.5
  201.8 2.8 %bitcast_convert_fusion.1 = bf16[512,768]{1,0:T(8,128)(2,1)} fusion(pred[4,136,512]{2,1,0:T(8,128)(4,1)} %broadcast_compare_fusion, bf16[2,136,768]{2,1,0:T(8,128)(2,1)} %collective-permute-done.2, f32[2,136]{1,0:T(2,128)S(1)} %slice.23, bf16[2,136,1536]{2,1,0:T(8,128)(2,1)} %copy-done.4, s32[]{:T(128)S(6)} %select_n.80), kind=kOutput, calls=%fused_computation.17 | convolution fusion | flops 215347200 | bytes 1762372 | tf_op jit(solution)/shard_map/dot_general | solution.py:108
  204.9 13.9 %convolution_convert_fusion = bf16[4,2048,1536]{2,1,0:T(8,128)(2,1)} fusion(bf16[4,136,2048]{2,1,0:T(8,128)(2,1)S(1)} %copy-done.2, bf16[4,136,1536]{2,1,0:T(8,128)(2,1)} %fusion), kind=kOutput, calls=%fused_computation | convolution fusion | flops 3435134976 | bytes 29065216 | tf_op jit(solution)/shard_map/pch,pcd->phd/dot_general | solution.py:115
  218.8 2.7 %bitcast_convert_fusion = bf16[512,768]{1,0:T(8,128)(2,1)} fusion(pred[4,136,512]{2,1,0:T(8,128)(4,1)} %broadcast_compare_fusion, bf16[2,136,768]{2,1,0:T(8,128)(2,1)} %collective-permute-done.5, bf16[2,136,1536]{2,1,0:T(8,128)(2,1)S(1)} %fusion.2, s32[]{:T(128)S(6)} %select_n.80), kind=kOutput, calls=%fused_computation.15 | convolution fusion | flops 215138304 | bytes 1761284 | tf_op jit(solution)/shard_map/dot_general | solution.py:108
  221.6 14.1 %convolution_convert_fusion.1 = bf16[4,1536,2048]{2,1,0:T(8,128)(2,1)} fusion(bf16[4,136,1536]{2,1,0:T(8,128)(2,1)S(1)} %bitcast.77, bf16[4,136,2048]{2,1,0:T(8,128)(2,1)} %all-gather.11.cloned.1.call-done), kind=kOutput, calls=%fused_computation.1 | convolution fusion | flops 3435134976 | bytes 29065216 | tf_op jit(solution)/shard_map/pcd,pch->pdh/dot_general | solution.py:116
  235.7 16.8 %reduce-scatter.5.cloned.1.call-done = bf16[128,768]{1,0:T(8,128)(2,1)} async-done(((bf16[512,768]{1,0:T(8,128)(2,1)}), bf16[128,768]{1,0:T(8,128)(2,1)}) %reduce-scatter.5.cloned.1.call-update) | async-done | bytes 196624 | tf_op jit(solution)/shard_map/reduce_scatter | solution.py:111
  (41 shorter events, 4.3 us)
Async XLA Ops:
  7.2 42.2 %all-gather.5.cloned.1.call-start = ((), (), s32[]{:S(2)}) async-start(), calls=%async_computation.2 | async-start | bytes 1966080 | tf_op jit(solution)/shard_map/all_gather | solution.py:67
  7.9 79.1 %all-gather.9.cloned.1.call-start = ((), (), s32[]{:S(2)}) async-start(), calls=%async_computation.5 | async-start | bytes 1966080 | tf_op jit(solution)/shard_map/all_gather | solution.py:68
  8.6 152.9 %all-gather.7.cloned.1.call-start = ((), (), s32[]{:S(2)}) async-start(), calls=%async_computation.3 | async-start | bytes 2785280 | tf_op jit(solution)/shard_map/all_gather | solution.py:42
  51.8 12.8 %copy-start = (bf16[544,1536]{1,0:T(8,128)(2,1)}, bf16[544,1536]{1,0:T(8,128)(2,1)S(1)}, u32[]{:S(2)}) copy-start(bf16[544,1536]{1,0:T(8,128)(2,1)S(1)} %convolution_convert_fusion.4) | copy-start | bytes 5013508
  64.8 42.9 %collective-permute-start = (bf16[2,1,136,2048]{3,2,1,0:T(8,128)(2,1)S(1)}, bf16[2,1,136,2048]{3,2,1,0:T(8,128)(2,1)}, u32[]{:S(2)}, u32[]{:S(2)}) collective-permute-start(bf16[2,1,136,2048]{3,2,1,0:T(8,128)(2,1)S(1)} %dynamic-slice_bitcast_fusion.1), channel_id=1, source_target_pairs={{0,4},{4,0},{8,12},{12,8},{1,5},{5,1},{9,13},{13,9},{2,6},{6,2},{1... | collective-permute-start | bytes 3342344 | tf_op jit(solution)/shard_map/ppermute | solution.py:18
  107.6 4.2 %collective-permute-start.3 = (bf16[2,1,136,2048]{3,2,1,0:T(8,128)(2,1)}, bf16[2,1,136,2048]{3,2,1,0:T(8,128)(2,1)}, u32[]{:S(2)}, u32[]{:S(2)}) collective-permute-start(bf16[2,1,136,2048]{3,2,1,0:T(8,128)(2,1)} %dynamic-slice_bitcast_fusion), channel_id=1, source_target_pairs={{0,4},{4,0},{8,12},{12,8},{1,5},{5,1},{9,13},{13,9},{2,6},{6,2},{1... | collective-permute-start | bytes 3342344 | tf_op jit(solution)/shard_map/ppermute | solution.py:18
  107.6 4.2 %copy-start.3 = (bf16[4,136,2048]{2,1,0:T(8,128)(2,1)S(1)}, bf16[4,136,2048]{2,1,0:T(8,128)(2,1)}, u32[]{:S(2)}) copy-start(bf16[4,136,2048]{2,1,0:T(8,128)(2,1)} %convolution_convert_fusion.2) | copy-start | bytes 6684676
  110.3 15.6 %collective-permute-start.1 = (bf16[1,136,2048]{2,1,0:T(8,128)(2,1)}, bf16[1,136,2048]{2,1,0:T(8,128)(2,1)S(1)}, u32[]{:S(2)}, u32[]{:S(2)}) collective-permute-start(bf16[1,136,2048]{2,1,0:T(8,128)(2,1)} %dynamic-slice_bitcast_fusion.3), channel_id=1, source_target_pairs={{0,8},{4,12},{8,0},{12,4},{1,9},{5,13},{9,1},{13,5},{2,10},{6,14},... | collective-permute-start | bytes 1671176 | tf_op jit(solution)/shard_map/ppermute | solution.py:18
  114.3 23.2 %collective-permute-start.4 = (bf16[1,136,2048]{2,1,0:T(8,128)(2,1)}, bf16[1,136,2048]{2,1,0:T(8,128)(2,1)S(1)}, u32[]{:S(2)}, u32[]{:S(2)}) collective-permute-start(bf16[1,136,2048]{2,1,0:T(8,128)(2,1)} %dynamic-slice_bitcast_fusion.2), channel_id=1, source_target_pairs={{0,8},{4,12},{8,0},{12,4},{1,9},{5,13},{9,1},{13,5},{2,10},{6,14},... | collective-permute-start | bytes 1671176 | tf_op jit(solution)/shard_map/ppermute | solution.py:18
  139.2 47.1 %all-gather.11.cloned.1.call-start = ((), (), s32[]{:S(2)}) async-start(), calls=%async_computation.6 | async-start | bytes 2785280 | tf_op jit(solution)/shard_map/all_gather | solution.py:42
  139.8 95.9 %reduce-scatter.3.cloned.1.call-start = ((), (), s32[]{:S(2)}) async-start(), calls=%async_computation.4 | async-start | bytes 983040 | tf_op jit(solution)/shard_map/reduce_scatter | solution.py:111
  174.4 0.9 copy-start.4
  176.1 25.6 %collective-permute-start.2 = (bf16[2,136,768]{2,1,0:T(8,128)(2,1)}, bf16[2,136,768]{2,1,0:T(8,128)(2,1)}, u32[]{:S(2)}, u32[]{:S(2)}) collective-permute-start(bf16[2,136,768]{2,1,0:T(8,128)(2,1)} %constant_dynamic-slice_fusion.1), channel_id=1, source_target_pairs={{0,16},{16,0},{1,17},{17,1},{2,18},{18,2},{3,19},{19,3},{4,20},{20... | collective-permute-start | bytes 1253384 | tf_op jit(solution)/shard_map/ppermute | solution.py:18
  200.2 4.7 %copy-start.2 = (bf16[4,136,2048]{2,1,0:T(8,128)(2,1)S(1)}, bf16[4,136,2048]{2,1,0:T(8,128)(2,1)}, u32[]{:S(2)}) copy-start(bf16[4,136,2048]{2,1,0:T(8,128)(2,1)} %all-gather.7.cloned.1.call-done) | copy-start | bytes 6684676
  200.2 18.6 %collective-permute-start.5 = (bf16[2,136,768]{2,1,0:T(8,128)(2,1)S(1)}, bf16[2,136,768]{2,1,0:T(8,128)(2,1)}, u32[]{:S(2)}, u32[]{:S(2)}) collective-permute-start(bf16[2,136,768]{2,1,0:T(8,128)(2,1)S(1)} %constant_dynamic-slice_fusion), channel_id=1, source_target_pairs={{0,16},{16,0},{1,17},{17,1},{2,18},{18,2},{3,19},{19,3},{4,20},{20... | collective-permute-start | bytes 1253384 | tf_op jit(solution)/shard_map/ppermute | solution.py:18
  204.6 47.9 %reduce-scatter.5.cloned.1.call-start = ((), (), s32[]{:S(2)}) async-start(), calls=%async_computation.7 | async-start | bytes 983040 | tf_op jit(solution)/shard_map/reduce_scatter | solution.py:111
  218.8 2.8 %copy-start.1 = (bf16[544,1536]{1,0:T(8,128)(2,1)S(1)}, bf16[544,1536]{1,0:T(8,128)(2,1)}, u32[]{:S(2)}) copy-start(bf16[544,1536]{1,0:T(8,128)(2,1)} %copy-done) | copy-start | bytes 5013508
Sparse Core Ops, SparseCore 0:
  9.6 39.7 all-gather.4
  51.0 35.9 all-gather.8
  139.3 22.1 all-gather.6
  162.9 23.3 all-gather.10
  204.7 22.4 reduce-scatter.2
  230.0 22.4 reduce-scatter.4

commit v2 on v1

v2 whole, which is shorter than its diff:
```python
import jax
import jax.numpy as jnp
from jax import lax
from jax.sharding import PartitionSpec as P

CAP = 34
BF = jnp.bfloat16
F32 = jnp.float32


def silu_slope(pre):
    sigma = jax.nn.sigmoid(pre)
    return sigma * (1.0 + pre * (1.0 - sigma))


def swap(value, axis, bit):
    count = lax.axis_size(axis)
    return lax.ppermute(value, axis, [(i, i ^ bit) for i in range(count)])


def pick(value, index, axis):
    return lax.dynamic_index_in_dim(value, index, axis, keepdims=False)


def near_sum(part):
    count = lax.axis_size("dp")
    pairs, rows, hidden = part.shape
    if count != 4 or pairs % 4:
        return part
    core = lax.axis_index("dp") % 2
    cut = part.reshape(2, 2, pairs // 4, rows, hidden)
    other = swap(pick(cut, 1 - core, 1), "dp", 1)
    return (pick(cut, core, 1).astype(F32) + other.astype(F32)).astype(BF)


def far_sum(near):
    if near.ndim == 3:
        return lax.psum_scatter(near, "dp", scatter_dimension=2, tiled=True).astype(F32)
    chip = lax.axis_index("dp") // 2
    far = swap(pick(near, 1 - chip, 0), "dp", 2)
    return pick(near, chip, 0).astype(F32) + far.astype(F32)


def in_order(mine, other, index):
    first = jnp.where(index == 0, mine, other)
    second = jnp.where(index == 0, other, mine)
    return first, second


def share_of_features(value, pairs):
    if lax.axis_size("dp") != 4 or pairs % 4:
        return lax.all_gather(value, "dp", axis=2, tiled=True)
    me = lax.axis_index("dp")
    core, chip = me % 2, me // 2
    near = swap(value, "dp", 1)
    far = swap(value, "dp", 2)
    far_near = swap(far, "dp", 1)
    low, high = in_order(value, near, core)
    far_low, far_high = in_order(far, far_near, core)
    a0, a1 = in_order(low, far_low, chip)
    b0, b1 = in_order(high, far_high, chip)
    return jnp.concatenate([a0, b0, a1, b1], axis=0)


def sum_over_hidden(part):
    count = lax.axis_size("pipe")
    part = part.astype(BF)
    if count != 2:
        return lax.psum_scatter(part, "pipe", scatter_dimension=2, tiled=True).astype(F32)
    me = lax.axis_index("pipe")
    width = part.shape[2] // 2
    sent = swap(lax.dynamic_slice_in_dim(part, (1 - me) * width, width, 2), "pipe", 1)
    return lax.dynamic_slice_in_dim(part, me * width, width, 2).astype(F32) + sent.astype(F32)


def shifted(value, by):
    count = lax.axis_size("expert")
    return lax.ppermute(value, "expert", [(i, (i + by) % count) for i in range(count)])


def all_features(value):
    if lax.axis_size("pipe") != 2:
        return lax.all_gather(value, "pipe", axis=1, tiled=True)
    other = swap(value, "pipe", 1)
    return jnp.concatenate(in_order(value, other, lax.axis_index("pipe")), axis=1)


def deliver(chunks):
    groups = lax.axis_size("expert")
    width = chunks.shape[2] // lax.axis_size("pipe")
    start = lax.axis_index("pipe") * width
    moved = [shifted(lax.dynamic_slice_in_dim(chunks[s], start, width, 1), s) for s in range(1, groups)]
    return jnp.concatenate([chunks[0]] + [all_features(part) for part in moved], axis=0)


def on_device(tokens, expert_ids, gates, w_up, w_down, cotangent):
    groups = lax.axis_size("expert")
    me = lax.axis_index("expert")
    pairs, features, hidden_width = w_up.shape
    halves = 2 if pairs % 2 == 0 else 1
    sets = pairs // halves
    rows = groups * CAP
    own = tokens.shape[0]
    slots = -(-sets * CAP // 8) * 8

    place = jnp.arange(groups * sets, dtype=jnp.int32)
    wanted = ((lax.rem(place // sets + me, groups) * pairs + lax.rem(place, sets) * halves) // 2)[:, None]
    first, second = expert_ids[:, 0][None, :] == wanted, expert_ids[:, 1][None, :] == wanted
    chosen = first | second
    before = jnp.arange(own)[:, None] < jnp.arange(own)[None, :]
    position = jnp.dot(chosen.astype(BF), before.astype(BF), preferred_element_type=F32).astype(jnp.int32)
    slot = jnp.where(chosen, position + lax.rem(place, sets)[:, None] * CAP, -1)
    slot = slot.reshape(groups, sets, 1, own)
    column = jnp.arange(slots, dtype=jnp.int32)[None, None, :, None]
    match = slot == column
    routing = jnp.any(match, axis=1)
    gate = jnp.where(first, gates[:, 0][None, :], 0.0) + jnp.where(second, gates[:, 1][None, :], 0.0)
    weighting = jnp.sum(jnp.where(match, gate.reshape(groups, sets, 1, own), 0.0), axis=1)
    slot_weight = jnp.sum(weighting, axis=2)
    routing = routing.astype(BF)

    def spread(array):
        return jnp.einsum("gst,td->gsd", routing, array, preferred_element_type=F32)

    target = jnp.arange(pairs * rows, dtype=jnp.int32)
    inside = lax.rem(target, rows)
    source = (inside // CAP) * slots + (target // (rows * halves)) * CAP + lax.rem(inside, CAP)
    order = (source[:, None] == jnp.arange(groups * slots, dtype=jnp.int32)[None, :]).astype(BF)
    set_order = order.reshape(sets, halves, rows, groups * slots)[:, 0].reshape(sets * rows, groups * slots)

    def by_pair(arrivals):
        placed = jnp.dot(order, arrivals, preferred_element_type=F32).astype(BF)
        return placed.reshape(pairs, rows, features)

    arrivals = deliver(spread(tokens).astype(BF))
    grad_arrivals = deliver((spread(cotangent) * slot_weight[:, :, None]).astype(BF))
    arrived = by_pair(arrivals)
    pre_part = jnp.einsum("pcd,pdh->pch", arrived, w_up, preferred_element_type=F32).astype(BF)
    pre_near = near_sum(pre_part)
    grad_rows, pre_near = lax.optimization_barrier((by_pair(grad_arrivals), pre_near))
    pre_share = far_sum(pre_near)
    grad_part = jnp.einsum("pcd,phd->pch", grad_rows, w_down, preferred_element_type=F32).astype(BF)

    hidden = share_of_features(jax.nn.silu(pre_share).astype(BF), pairs)
    grad_share = far_sum(near_sum(grad_part))
    grad_pre = share_of_features((grad_share * silu_slope(pre_share)).astype(BF), pairs)

    def by_set(value):
        return value.reshape((sets, halves) + value.shape[1:])

    def back_to_tokens(summed):
        flat = summed.astype(BF).reshape(sets * rows, summed.shape[2])
        chunks = lax.dot_general(set_order, flat, (((0,), (0,)), ((), ())), preferred_element_type=F32)
        chunks = chunks.astype(BF).reshape(groups, slots, summed.shape[2])
        moved = [chunks[0]] + [shifted(chunks[s], groups - s) for s in range(1, groups)]
        return jnp.concatenate(moved, axis=0)

    out_part = jnp.einsum("rhck,rhkd->rcd", by_set(hidden), by_set(w_down), preferred_element_type=F32)
    out_home = back_to_tokens(sum_over_hidden(out_part))
    output = lax.dot_general(
        weighting.reshape(groups * slots, own), out_home.astype(F32),
        (((0,), (0,)), ((), ())), precision=lax.Precision.HIGHEST,
    ).astype(BF)
    down_grad = jnp.einsum("pch,pcd->phd", hidden, grad_rows, preferred_element_type=F32).astype(BF)
    grad_pre, down_grad = lax.optimization_barrier((grad_pre, down_grad))
    back_part = jnp.einsum("rhck,rhdk->rcd", by_set(grad_pre), by_set(w_up), preferred_element_type=F32)
    back_part, late = lax.optimization_barrier((back_part.astype(BF), grad_pre))
    back_home = back_to_tokens(sum_over_hidden(back_part))
    token_grad = lax.dot_general(
        routing.reshape(groups * slots, own), back_home, (((0,), (0,)), ((), ())),
        preferred_element_type=F32,
    ).astype(BF)
    up_grad = jnp.einsum("pcd,pch->pdh", arrived, late, preferred_element_type=F32).astype(BF)
    return (output, token_grad, up_grad, down_grad)


def solution(mesh):
    return jax.shard_map(
        on_device,
        mesh=mesh,
        in_specs=(
            P("expert", "dp"),
            P("expert", None),
            P("expert", None),
            P("expert", "dp", "pipe"),
            P("expert", "pipe", "dp"),
            P("expert", "dp"),
        ),
        out_specs=(
            P("expert", ("dp", "pipe")),
            P("expert", ("dp", "pipe")),
            P("expert", "dp", "pipe"),
            P("expert", "pipe", "dp"),
        ),
        check_vma=False,
    )
```

time: 260 us -> 221 us (0.85)
  waiting for transfers between devices: 118 us -> 72.5 us
  starting transfers between devices: 5.64 us -> 36.4 us
  blocking collectives: 13.5 us -> 0 us
  between operations: 14.3 us -> 1 us
  matrix products: 93.9 us -> 86.4 us
  other arithmetic: 8.05 us -> 13.2 us
  local copies, waits for them, and re-layouts: 6.12 us -> 11 us
    all_gather x4 -> x0, waiting for transfers between devices: 76.3 us -> none  [the longest x2 29.4 us: share_of_features(): return lax.all_gather(value, 'dp', axis=0, tiled=True)]
    ppermute x6 -> x18, waiting for transfers between devices: 22.6 us -> 57.1 us  [swap(): return lax.ppermute(value, axis, [(i, i ^ bit) for i in range(count)])]
    ppermute x0 -> x12, starting transfers between devices: none -> 21.9 us  [shifted(): lax.ppermute(value, 'expert', [(i, (i + by) % count) for i in range(count)])]
    reduce_scatter x2 -> x0, waiting for transfers between devices: 16.8 us -> none  [home(): lax.psum_scatter(placed.astype(BF), 'expert', scatter_dimension=0, tiled=...]
    ppermute x0 -> x12, waiting for transfers between devices: none -> 15.4 us  [shifted(): lax.ppermute(value, 'expert', [(i, (i + by) % count) for i in range(count)])]
    all_gather x1 -> x0, blocking collectives: 13.5 us -> none  [on_device(): meta = lax.all_gather(meta, 'expert', axis=1, tiled=True)]
    ppermute x6 -> x18, starting transfers between devices: 5.01 us -> 14.4 us  [swap(): return lax.ppermute(value, axis, [(i, i ^ bit) for i in range(count)])]
    dot_general x5 -> x9, matrix products: 25.7 us -> 21.4 us  [the longest x1 14.1 us: on_device(): jnp.einsum('pcd,pch->pdh', arrived, late, preferred_element_type=F32)]
  transfers between devices with their start and end apart: 12 -> 30, of which waited for: 7 -> 12; matrix products, arithmetic and copies ran while one was open for 41% -> 38% of each run, Pallas kernels for 0% -> 0%
where the time goes in v2:
time: 221 us
  matrix products  86.4 us (39%)
  waiting for transfers between devices  72.5 us (33%)
  starting transfers between devices  36.4 us (16%)
  other arithmetic  13.2 us (6%)
  local copies, waits for them, and re-layouts  11 us (5%)
    ppermute x18, waiting for transfers between devices, swap(): return lax.ppermute(value, axis, [(i, i ^ bit) for i in range(count)])  57.1 us
    ppermute x12, starting transfers between devices, shifted(): lax.ppermute(value, 'expert', [(i, (i + by) % count) for i in range(count)])  21.9 us
    ppermute x12, waiting for transfers between devices, shifted(): lax.ppermute(value, 'expert', [(i, (i + by) % count) for i in range(count)])  15.4 us
    dot_general x1, matrix products, on_device(): jnp.einsum('rhck,rhdk->rcd', by_set(grad_pre), by_set(w_up), preferred_el...  14.7 us
    ppermute x18, starting transfers between devices, swap(): return lax.ppermute(value, axis, [(i, i ^ bit) for i in range(count)])  14.4 us
    dot_general x1, matrix products, on_device(): jnp.einsum('pcd,pch->pdh', arrived, late, preferred_element_type=F32)  14.1 us
    dot_general x1, matrix products, on_device(): jnp.einsum('pch,pcd->phd', hidden, grad_rows, preferred_element_type=F32)  13.8 us
    dot_general x1, matrix products, on_device(): jnp.einsum('pcd,phd->pch', grad_rows, w_down, preferred_element_type=F32)  13.5 us
  transfers between devices with their start and end apart: 30, of which 12 were waited for; matrix products, arithmetic and copies ran while one was open for 38% of the time, Pallas kernels for 0%

profile of v2, /device:TPU:0, one launch (start us, length us, event | category | flops | bytes accessed | tf_op | source)
XLA Modules:
  0.0 220.5 jit_solution(7479143052031183657)
XLA Ops:
  3.7 3.1 %collective-permute-start = (bf16[72,768]{1,0:T(8,128)(2,1)S(1)}, bf16[72,768]{1,0:T(8,128)(2,1)S(1)}, u32[]{:S(2)}, u32[]{:S(2)}) collective-permute-start(bf16[72,768]{1,0:T(8,128)(2,1)S(1)} %dynamic-slice_bitcast_fusion.9), channel_id=1, source_target_pairs={{0,1},{1,2},{2,3},{3,0},{4,5},{5,6},{6,7},{7,4},{8,9},{9,10},{10,1... | collective-permute-start | bytes 331784 | tf_op jit(solution)/shard_map/ppermute | solution.py:78
  6.8 2.7 %collective-permute-start.2 = (bf16[72,768]{1,0:T(8,128)(2,1)S(1)}, bf16[72,768]{1,0:T(8,128)(2,1)S(1)}, u32[]{:S(2)}, u32[]{:S(2)}) collective-permute-start(bf16[72,768]{1,0:T(8,128)(2,1)S(1)} %dynamic-slice_bitcast_fusion.8), channel_id=1, source_target_pairs={{0,2},{1,3},{2,0},{3,1},{4,6},{5,7},{6,4},{7,5},{8,10},{9,11},{10,... | collective-permute-start | bytes 331784 | tf_op jit(solution)/shard_map/ppermute | solution.py:78
  10.0 2.0 collective-permute-start.8
  12.0 2.0 collective-permute-start.10
  14.6 3.2 %collective-permute-done.6 = bf16[72,768]{1,0:T(8,128)(2,1)S(1)} collective-permute-done((bf16[72,768]{1,0:T(8,128)(2,1)S(1)}, bf16[72,768]{1,0:T(8,128)(2,1)S(1)}, u32[]{:S(2)}, u32[]{:S(2)}) %collective-permute-start.6) | collective-permute-done | bytes 110624 | tf_op jit(solution)/shard_map/ppermute | solution.py:78
  19.4 4.4 %collective-permute-done.8 = bf16[72,768]{1,0:T(8,128)(2,1)S(1)} collective-permute-done((bf16[72,768]{1,0:T(8,128)(2,1)S(1)}, bf16[72,768]{1,0:T(8,128)(2,1)S(1)}, u32[]{:S(2)}, u32[]{:S(2)}) %collective-permute-start.8) | collective-permute-done | bytes 110624 | tf_op jit(solution)/shard_map/ppermute | solution.py:78
  27.4 4.8 %collective-permute-done.9 = bf16[72,768]{1,0:T(8,128)(2,1)S(1)} collective-permute-done((bf16[72,768]{1,0:T(8,128)(2,1)S(1)}, bf16[72,768]{1,0:T(8,128)(2,1)S(1)}, u32[]{:S(2)}, u32[]{:S(2)}) %collective-permute-start.9) | collective-permute-done | bytes 110624 | tf_op jit(solution)/shard_map/ppermute | solution.py:18
  34.6 12.4 %convolution_convert_fusion.3 = bf16[4,136,2048]{2,1,0:T(8,128)(2,1)S(1)} fusion(bf16[4,136,1536]{2,1,0:T(8,128)(2,1)S(1)} %bitcast.102, bf16[4,1536,2048]{2,1,0:T(8,128)(2,1)} %param.9), kind=kOutput, calls=%fused_computation.3 | convolution fusion | flops 3423666176 | bytes 29065216 | tf_op jit(solution)/shard_map/pcd,pdh->pch/dot_general | solution.py:138
  50.1 3.8 %collective-permute-done.3 = bf16[72,768]{1,0:T(8,128)(2,1)S(1)} collective-permute-done((bf16[72,768]{1,0:T(8,128)(2,1)S(1)}, bf16[72,768]{1,0:T(8,128)(2,1)S(1)}, u32[]{:S(2)}, u32[]{:S(2)}) %collective-permute-start.3) | collective-permute-done | bytes 110624 | tf_op jit(solution)/shard_map/ppermute | solution.py:18
  54.0 2.0 collective-permute-done.5
  56.0 2.3 %convolution_convert_fusion.5 = bf16[544,1536]{1,0:T(8,128)(2,1)} fusion(bf16[72,768]{1,0:T(8,128)(2,1)S(1)} %get-tuple-element.55, bf16[72,768]{1,0:T(8,128)(2,1)S(1)} %get-tuple-element.54, bf16[72,768]{1,0:T(8,128)(2,1)S(1)} %get-tuple-element.53, bf16[72,768]{1,0:T(8,128)(2,1)S(1)} %get-tuple-element.52, bf16[72,768]{1,0:T(8,128)(2,1)S(1)} %get-tuple-element.51, ...), kind=kOutput, calls=%fused_computation.5 | convolution fusion | flops 488481792 | bytes 2558080 | tf_op jit(solution)/shard_map/dot_general | solution.py:132
  58.2 2.7 %fusion.4 = bf16[2,1,136,2048]{3,2,1,0:T(8,128)(2,1)} fusion(bf16[2,1,136,2048]{3,2,1,0:T(8,128)(2,1)} %collective-permute-done.12, bf16[2,2,1,136,2048]{4,3,1,0,2:T(8,128)(2,1)S(1)} %bitcast.101, s32[]{:T(128)S(6)} %select_n.279), kind=kLoop, calls=%fused_computation.18 | loop fusion | flops 2228224 | bytes 3342340 | tf_op jit(solution)/shard_map/convert_element_type | solution.py:33
  60.9 13.5 %convolution_convert_fusion.2 = bf16[4,136,2048]{2,1,0:T(8,128)(2,1)S(1)} fusion(bf16[4,136,1536]{2,1,0:T(8,128)(2,1)} %bitcast.108, bf16[4,2048,1536]{2,1,0:T(8,128)(2,1)} %param.10), kind=kOutput, calls=%fused_computation.2 | convolution fusion | flops 3423666176 | bytes 29065216 | tf_op jit(solution)/shard_map/pcd,phd->pch/dot_general | solution.py:142
  75.5 1.9 dynamic-slice_bitcast_fusion.3
  82.9 10.2 %collective-permute-done.13 = bf16[1,136,2048]{2,1,0:T(8,128)(2,1)S(1)} collective-permute-done((bf16[1,136,2048]{2,1,0:T(8,128)(2,1)}, bf16[1,136,2048]{2,1,0:T(8,128)(2,1)S(1)}, u32[]{:S(2)}, u32[]{:S(2)}) %collective-permute-start.13) | collective-permute-done | bytes 557088 | tf_op jit(solution)/shard_map/ppermute | solution.py:18
  93.1 11.6 %collective-permute-done.22 = bf16[1,136,2048]{2,1,0:T(8,128)(2,1)S(1)} collective-permute-done((bf16[1,136,2048]{2,1,0:T(8,128)(2,1)S(1)}, bf16[1,136,2048]{2,1,0:T(8,128)(2,1)S(1)}, u32[]{:S(2)}, u32[]{:S(2)}) %collective-permute-start.22) | collective-permute-done | bytes 557088 | tf_op jit(solution)/shard_map/ppermute | solution.py:18
  104.6 2.7 %fusion.6 = (bf16[1,136,2048]{2,1,0:T(8,128)(2,1)}, bf16[1,136,2048]{2,1,0:T(8,128)(2,1)S(1)}) fusion(bf16[1,136,2048]{2,1,0:T(8,128)(2,1)S(1)} %collective-permute-done.22, bf16[1,136,2048]{2,1,0:T(8,128)(2,1)S(1)} %collective-permute-done.13, bf16[2,1,136,2048]{3,2,1,0:T(8,128)(2,1)} %copy-done.9, s32[]{:T(128)S(6)} %select_n.281, ...), kind=kLoop, calls=%fused_computation.25 | loop fusion | flops 4734976 | bytes 3342340 | tf_op jit(solution)/shard_map/convert_element_type | solution.py:146
  109.3 13.5 %collective-permute-done.15 = bf16[1,136,2048]{2,1,0:T(8,128)(2,1)S(1)} collective-permute-done((bf16[1,136,2048]{2,1,0:T(8,128)(2,1)S(1)}, bf16[1,136,2048]{2,1,0:T(8,128)(2,1)S(1)}, u32[]{:S(2)}, u32[]{:S(2)}) %collective-permute-start.15) | collective-permute-done | bytes 557088 | tf_op jit(solution)/shard_map/ppermute | solution.py:18
  123.6 10.0 %collective-permute-done.24 = bf16[1,136,2048]{2,1,0:T(8,128)(2,1)} collective-permute-done((bf16[1,136,2048]{2,1,0:T(8,128)(2,1)}, bf16[1,136,2048]{2,1,0:T(8,128)(2,1)}, u32[]{:S(2)}, u32[]{:S(2)}) %collective-permute-start.24) | collective-permute-done | bytes 557088 | tf_op jit(solution)/shard_map/ppermute | solution.py:18
  134.9 10.4 %fusion.1 = bf16[2,136,1536]{2,1,0:T(8,128)(2,1)S(1)} fusion(bf16[2,2,136,2048]{3,2,1,0:T(8,128)(2,1)S(1)} %bitcast.105, bf16[2,2,2048,1536]{3,2,1,0:T(8,128)(2,1)} %bitcast.98), kind=kOutput, calls=%fused_computation.11 | convolution fusion | flops 3422969856 | bytes 28229632 | tf_op jit(solution)/shard_map/rhck,rhkd->rcd/dot_general | solution.py:158
  145.3 13.8 %convolution_convert_fusion.1 = bf16[4,2048,1536]{2,1,0:T(8,128)(2,1)} fusion(bf16[4,136,1536]{2,1,0:T(8,128)(2,1)S(1)} %bitcast.109, bf16[1,136,2048]{2,1,0:T(8,128)(2,1)} %copy-done.8, bf16[1,136,2048]{2,1,0:T(8,128)(2,1)} %copy-done.7, bf16[1,136,2048]{2,1,0:T(8,128)(2,1)} %copy-done.6, bf16[1,136,2048]{2,1,0:T(8,128)(2,1)S(1)} %get-tuple-element.22), kind=kOutput, calls=%fused_computation.1 | convolution fusion | flops 3438477312 | bytes 29065216 | tf_op jit(solution)/shard_map/pch,pcd->phd/dot_general | solution.py:164
  161.4 1.7 broadcast_select_fusion.11
  163.2 1.7 pad_maximum_fusion.1
  164.8 14.7 %fusion.2 = bf16[2,136,1536]{2,1,0:T(8,128)(2,1)} fusion(bf16[2,2,136,2048]{3,2,1,0:T(8,128)(2,1)} %bitcast.104, bf16[2,2,1536,2048]{3,2,1,0:T(8,128)(2,1)} %bitcast.99), kind=kOutput, calls=%fused_computation.12 | convolution fusion | flops 3422969856 | bytes 28229632 | tf_op jit(solution)/shard_map/rhck,rhdk->rcd/dot_general | solution.py:166
  179.6 1.8 constant_dynamic-slice_fusion
  181.9 14.1 %convolution_convert_fusion = bf16[4,1536,2048]{2,1,0:T(8,128)(2,1)} fusion(bf16[4,136,1536]{2,1,0:T(8,128)(2,1)S(1)} %bitcast.103, bf16[4,136,2048]{2,1,0:T(8,128)(2,1)} %pad_maximum_fusion.1), kind=kOutput, calls=%fused_computation | convolution fusion | flops 3435134976 | bytes 29065216 | tf_op jit(solution)/shard_map/pcd,pch->pdh/dot_general | solution.py:173
  196.7 3.7 %collective-permute-start.20 = (bf16[72,768]{1,0:T(8,128)(2,1)S(1)}, bf16[72,768]{1,0:T(8,128)(2,1)S(1)}, u32[]{:S(2)}, u32[]{:S(2)}) collective-permute-start(bf16[72,768]{1,0:T(8,128)(2,1)S(1)} %get-tuple-element.41), channel_id=1, source_target_pairs={{0,1},{1,2},{2,3},{3,0},{4,5},{5,6},{6,7},{7,4},{8,9},{9,10},{10,1... | collective-permute-start | bytes 331784 | tf_op jit(solution)/shard_map/ppermute | solution.py:78
  200.4 2.2 %collective-permute-start.19 = (bf16[72,768]{1,0:T(8,128)(2,1)S(1)}, bf16[72,768]{1,0:T(8,128)(2,1)S(1)}, u32[]{:S(2)}, u32[]{:S(2)}) collective-permute-start(bf16[72,768]{1,0:T(8,128)(2,1)S(1)} %get-tuple-element.42), channel_id=1, source_target_pairs={{0,2},{1,3},{2,0},{3,1},{4,6},{5,7},{6,4},{7,5},{8,10},{9,11},{10,... | collective-permute-start | bytes 331784 | tf_op jit(solution)/shard_map/ppermute | solution.py:78
  202.6 2.3 %collective-permute-start.18 = (bf16[72,768]{1,0:T(8,128)(2,1)S(1)}, bf16[72,768]{1,0:T(8,128)(2,1)S(1)}, u32[]{:S(2)}, u32[]{:S(2)}) collective-permute-start(bf16[72,768]{1,0:T(8,128)(2,1)S(1)} %get-tuple-element.43), channel_id=1, source_target_pairs={{0,3},{1,0},{2,1},{3,2},{4,7},{5,4},{6,5},{7,6},{8,11},{9,8},{10,9... | collective-permute-start | bytes 331784 | tf_op jit(solution)/shard_map/ppermute | solution.py:78
  207.2 3.3 %collective-permute-start.27 = (bf16[72,768]{1,0:T(8,128)(2,1)S(1)}, bf16[72,768]{1,0:T(8,128)(2,1)S(1)}, u32[]{:S(2)}, u32[]{:S(2)}) collective-permute-start(bf16[72,768]{1,0:T(8,128)(2,1)S(1)} %get-tuple-element.39), channel_id=1, source_target_pairs={{0,3},{1,0},{2,1},{3,2},{4,7},{5,4},{6,5},{7,6},{8,11},{9,8},{10,9... | collective-permute-start | bytes 331784 | tf_op jit(solution)/shard_map/ppermute | solution.py:78
  211.7 2.7 %collective-permute-done.29 = bf16[72,768]{1,0:T(8,128)(2,1)S(1)} collective-permute-done((bf16[72,768]{1,0:T(8,128)(2,1)S(1)}, bf16[72,768]{1,0:T(8,128)(2,1)S(1)}, u32[]{:S(2)}, u32[]{:S(2)}) %collective-permute-start.29) | collective-permute-done | bytes 110624 | tf_op jit(solution)/shard_map/ppermute | solution.py:78
  214.4 5.1 %collective-permute-done.28 = bf16[72,768]{1,0:T(8,128)(2,1)S(1)} collective-permute-done((bf16[72,768]{1,0:T(8,128)(2,1)S(1)}, bf16[72,768]{1,0:T(8,128)(2,1)S(1)}, u32[]{:S(2)}, u32[]{:S(2)}) %collective-permute-start.28) | collective-permute-done | bytes 110624 | tf_op jit(solution)/shard_map/ppermute | solution.py:78
  (109 shorter events, 33.5 us)
Async XLA Ops:
  3.7 15.6 %collective-permute-start = (bf16[72,768]{1,0:T(8,128)(2,1)S(1)}, bf16[72,768]{1,0:T(8,128)(2,1)S(1)}, u32[]{:S(2)}, u32[]{:S(2)}) collective-permute-start(bf16[72,768]{1,0:T(8,128)(2,1)S(1)} %dynamic-slice_bitcast_fusion.9), channel_id=1, source_target_pairs={{0,1},{1,2},{2,3},{3,0},{4,5},{5,6},{6,7},{7,4},{8,9},{9,10},{10,1... | collective-permute-start | bytes 331784 | tf_op jit(solution)/shard_map/ppermute | solution.py:78
  6.8 41.3 %collective-permute-start.2 = (bf16[72,768]{1,0:T(8,128)(2,1)S(1)}, bf16[72,768]{1,0:T(8,128)(2,1)S(1)}, u32[]{:S(2)}, u32[]{:S(2)}) collective-permute-start(bf16[72,768]{1,0:T(8,128)(2,1)S(1)} %dynamic-slice_bitcast_fusion.8), channel_id=1, source_target_pairs={{0,2},{1,3},{2,0},{3,1},{4,6},{5,7},{6,4},{7,5},{8,10},{9,11},{10,... | collective-permute-start | bytes 331784 | tf_op jit(solution)/shard_map/ppermute | solution.py:78
  9.9 7.9 %collective-permute-start.6 = (bf16[72,768]{1,0:T(8,128)(2,1)S(1)}, bf16[72,768]{1,0:T(8,128)(2,1)S(1)}, u32[]{:S(2)}, u32[]{:S(2)}) collective-permute-start(bf16[72,768]{1,0:T(8,128)(2,1)S(1)} %dynamic-slice_bitcast_fusion.6), channel_id=1, source_target_pairs={{0,1},{1,2},{2,3},{3,0},{4,5},{5,6},{6,7},{7,4},{8,9},{9,10},{10,1... | collective-permute-start | bytes 331784 | tf_op jit(solution)/shard_map/ppermute | solution.py:78
  10.0 13.8 %collective-permute-start.8 = (bf16[72,768]{1,0:T(8,128)(2,1)S(1)}, bf16[72,768]{1,0:T(8,128)(2,1)S(1)}, u32[]{:S(2)}, u32[]{:S(2)}) collective-permute-start(bf16[72,768]{1,0:T(8,128)(2,1)S(1)} %dynamic-slice_bitcast_fusion.5), channel_id=1, source_target_pairs={{0,2},{1,3},{2,0},{3,1},{4,6},{5,7},{6,4},{7,5},{8,10},{9,11},{10,... | collective-permute-start | bytes 331784 | tf_op jit(solution)/shard_map/ppermute | solution.py:78
  12.0 13.3 %collective-permute-start.10 = (bf16[72,768]{1,0:T(8,128)(2,1)S(1)}, bf16[72,768]{1,0:T(8,128)(2,1)S(1)}, u32[]{:S(2)}, u32[]{:S(2)}) collective-permute-start(bf16[72,768]{1,0:T(8,128)(2,1)S(1)} %dynamic-slice_bitcast_fusion.4), channel_id=1, source_target_pairs={{0,3},{1,0},{2,1},{3,2},{4,7},{5,4},{6,5},{7,6},{8,11},{9,8},{10,9... | collective-permute-start | bytes 331784 | tf_op jit(solution)/shard_map/ppermute | solution.py:78
  17.8 8.0 %collective-permute-start.7 = (bf16[72,768]{1,0:T(8,128)(2,1)S(1)}, bf16[72,768]{1,0:T(8,128)(2,1)S(1)}, u32[]{:S(2)}, u32[]{:S(2)}) collective-permute-start(bf16[72,768]{1,0:T(8,128)(2,1)S(1)} %collective-permute-done.6), channel_id=1, source_target_pairs={{0,16},{16,0},{1,17},{17,1},{2,18},{18,2},{3,19},{19,3},{4,20},{20... | collective-permute-start | bytes 331784 | tf_op jit(solution)/shard_map/ppermute | solution.py:18
  19.4 30.2 %collective-permute-start.4 = (bf16[72,768]{1,0:T(8,128)(2,1)}, bf16[72,768]{1,0:T(8,128)(2,1)S(1)}, u32[]{:S(2)}, u32[]{:S(2)}) collective-permute-start(bf16[72,768]{1,0:T(8,128)(2,1)} %dynamic-slice_bitcast_fusion.7), channel_id=1, source_target_pairs={{0,3},{1,0},{2,1},{3,2},{4,7},{5,4},{6,5},{7,6},{8,11},{9,8},{10,9... | collective-permute-start | bytes 331784 | tf_op jit(solution)/shard_map/ppermute | solution.py:78
  23.8 26.3 %collective-permute-start.1 = (bf16[72,768]{1,0:T(8,128)(2,1)S(1)}, bf16[72,768]{1,0:T(8,128)(2,1)S(1)}, u32[]{:S(2)}, u32[]{:S(2)}) collective-permute-start(bf16[72,768]{1,0:T(8,128)(2,1)S(1)} %collective-permute-done), channel_id=1, source_target_pairs={{0,16},{16,0},{1,17},{17,1},{2,18},{18,2},{3,19},{19,3},{4,20},{20... | collective-permute-start | bytes 331784 | tf_op jit(solution)/shard_map/ppermute | solution.py:18
  25.3 6.8 %collective-permute-start.9 = (bf16[72,768]{1,0:T(8,128)(2,1)S(1)}, bf16[72,768]{1,0:T(8,128)(2,1)S(1)}, u32[]{:S(2)}, u32[]{:S(2)}) collective-permute-start(bf16[72,768]{1,0:T(8,128)(2,1)S(1)} %collective-permute-done.8), channel_id=1, source_target_pairs={{0,16},{16,0},{1,17},{17,1},{2,18},{18,2},{3,19},{19,3},{4,20},{20... | collective-permute-start | bytes 331784 | tf_op jit(solution)/shard_map/ppermute | solution.py:18
  25.9 7.6 %collective-permute-start.11 = (bf16[72,768]{1,0:T(8,128)(2,1)S(1)}, bf16[72,768]{1,0:T(8,128)(2,1)S(1)}, u32[]{:S(2)}, u32[]{:S(2)}) collective-permute-start(bf16[72,768]{1,0:T(8,128)(2,1)S(1)} %collective-permute-done.10), channel_id=1, source_target_pairs={{0,16},{16,0},{1,17},{17,1},{2,18},{18,2},{3,19},{19,3},{4,20},{20... | collective-permute-start | bytes 331784 | tf_op jit(solution)/shard_map/ppermute | solution.py:18
  48.1 10.1 %collective-permute-start.12 = (bf16[2,1,136,2048]{3,2,1,0:T(8,128)(2,1)}, bf16[2,1,136,2048]{3,2,1,0:T(8,128)(2,1)}, u32[]{:S(2)}, u32[]{:S(2)}) collective-permute-start(bf16[2,1,136,2048]{3,2,1,0:T(8,128)(2,1)} %dynamic-slice_bitcast_fusion.1), channel_id=1, source_target_pairs={{0,4},{4,0},{8,12},{12,8},{1,5},{5,1},{9,13},{13,9},{2,6},{6,2},{1... | collective-permute-start | bytes 3342344 | tf_op jit(solution)/shard_map/ppermute | solution.py:18
  48.1 5.9 %collective-permute-start.3 = (bf16[72,768]{1,0:T(8,128)(2,1)S(1)}, bf16[72,768]{1,0:T(8,128)(2,1)S(1)}, u32[]{:S(2)}, u32[]{:S(2)}) collective-permute-start(bf16[72,768]{1,0:T(8,128)(2,1)S(1)} %collective-permute-done.2), channel_id=1, source_target_pairs={{0,16},{16,0},{1,17},{17,1},{2,18},{18,2},{3,19},{19,3},{4,20},{20... | collective-permute-start | bytes 331784 | tf_op jit(solution)/shard_map/ppermute | solution.py:18
  49.6 6.3 %collective-permute-start.5 = (bf16[72,768]{1,0:T(8,128)(2,1)S(1)}, bf16[72,768]{1,0:T(8,128)(2,1)S(1)}, u32[]{:S(2)}, u32[]{:S(2)}) collective-permute-start(bf16[72,768]{1,0:T(8,128)(2,1)S(1)} %collective-permute-done.4), channel_id=1, source_target_pairs={{0,16},{16,0},{1,17},{17,1},{2,18},{18,2},{3,19},{19,3},{4,20},{20... | collective-permute-start | bytes 331784 | tf_op jit(solution)/shard_map/ppermute | solution.py:18
  75.5 3.4 %collective-permute-start.21 = (bf16[2,1,136,2048]{3,2,1,0:T(8,128)(2,1)}, bf16[2,1,136,2048]{3,2,1,0:T(8,128)(2,1)}, u32[]{:S(2)}, u32[]{:S(2)}) collective-permute-start(bf16[2,1,136,2048]{3,2,1,0:T(8,128)(2,1)} %dynamic-slice_bitcast_fusion), channel_id=1, source_target_pairs={{0,4},{4,0},{8,12},{12,8},{1,5},{5,1},{9,13},{13,9},{2,6},{6,2},{1... | collective-permute-start | bytes 3342344 | tf_op jit(solution)/shard_map/ppermute | solution.py:18
  77.4 15.6 %collective-permute-start.13 = (bf16[1,136,2048]{2,1,0:T(8,128)(2,1)}, bf16[1,136,2048]{2,1,0:T(8,128)(2,1)S(1)}, u32[]{:S(2)}, u32[]{:S(2)}) collective-permute-start(bf16[1,136,2048]{2,1,0:T(8,128)(2,1)} %dynamic-slice_bitcast_fusion.3), channel_id=1, source_target_pairs={{0,8},{4,12},{8,0},{12,4},{1,9},{5,13},{9,1},{13,5},{2,10},{6,14},... | collective-permute-start | bytes 1671176 | tf_op jit(solution)/shard_map/ppermute | solution.py:18
  81.6 23.0 %collective-permute-start.22 = (bf16[1,136,2048]{2,1,0:T(8,128)(2,1)S(1)}, bf16[1,136,2048]{2,1,0:T(8,128)(2,1)S(1)}, u32[]{:S(2)}, u32[]{:S(2)}) collective-permute-start(bf16[1,136,2048]{2,1,0:T(8,128)(2,1)S(1)} %dynamic-slice_bitcast_fusion.2), channel_id=1, source_target_pairs={{0,8},{4,12},{8,0},{12,4},{1,9},{5,13},{9,1},{13,5},{2,10},{6,14},... | collective-permute-start | bytes 1671176 | tf_op jit(solution)/shard_map/ppermute | solution.py:18
  107.3 15.5 %collective-permute-start.15 = (bf16[1,136,2048]{2,1,0:T(8,128)(2,1)S(1)}, bf16[1,136,2048]{2,1,0:T(8,128)(2,1)S(1)}, u32[]{:S(2)}, u32[]{:S(2)}) collective-permute-start(bf16[1,136,2048]{2,1,0:T(8,128)(2,1)S(1)} %get-tuple-element.27), channel_id=1, source_target_pairs={{0,8},{4,12},{8,0},{12,4},{1,9},{5,13},{9,1},{13,5},{2,10},{6,14},... | collective-permute-start | bytes 1671176 | tf_op jit(solution)/shard_map/ppermute | solution.py:18
  108.8 24.8 %collective-permute-start.24 = (bf16[1,136,2048]{2,1,0:T(8,128)(2,1)}, bf16[1,136,2048]{2,1,0:T(8,128)(2,1)}, u32[]{:S(2)}, u32[]{:S(2)}) collective-permute-start(bf16[1,136,2048]{2,1,0:T(8,128)(2,1)} %get-tuple-element.26), channel_id=1, source_target_pairs={{0,8},{4,12},{8,0},{12,4},{1,9},{5,13},{9,1},{13,5},{2,10},{6,14},... | collective-permute-start | bytes 1671176 | tf_op jit(solution)/shard_map/ppermute | solution.py:18
  109.3 24.3 %collective-permute-start.14 = (bf16[1,136,2048]{2,1,0:T(8,128)(2,1)S(1)}, bf16[1,136,2048]{2,1,0:T(8,128)(2,1)S(1)}, u32[]{:S(2)}, u32[]{:S(2)}) collective-permute-start(bf16[1,136,2048]{2,1,0:T(8,128)(2,1)S(1)} %get-tuple-element.27), channel_id=1, source_target_pairs={{0,4},{4,0},{8,12},{12,8},{1,5},{5,1},{9,13},{13,9},{2,6},{6,2},{1... | collective-permute-start | bytes 1671176 | tf_op jit(solution)/shard_map/ppermute | solution.py:18
  122.8 10.8 %collective-permute-start.16 = (bf16[1,136,2048]{2,1,0:T(8,128)(2,1)S(1)}, bf16[1,136,2048]{2,1,0:T(8,128)(2,1)S(1)}, u32[]{:S(2)}, u32[]{:S(2)}) collective-permute-start(bf16[1,136,2048]{2,1,0:T(8,128)(2,1)S(1)} %collective-permute-done.15), channel_id=1, source_target_pairs={{0,4},{4,0},{8,12},{12,8},{1,5},{5,1},{9,13},{13,9},{2,6},{6,2},{1... | collective-permute-start | bytes 1671176 | tf_op jit(solution)/shard_map/ppermute | solution.py:18
  123.0 38.4 %collective-permute-start.23 = (bf16[1,136,2048]{2,1,0:T(8,128)(2,1)}, bf16[1,136,2048]{2,1,0:T(8,128)(2,1)}, u32[]{:S(2)}, u32[]{:S(2)}) collective-permute-start(bf16[1,136,2048]{2,1,0:T(8,128)(2,1)} %get-tuple-element.26), channel_id=1, source_target_pairs={{0,4},{4,0},{8,12},{12,8},{1,5},{5,1},{9,13},{13,9},{2,6},{6,2},{1... | collective-permute-start | bytes 1671176 | tf_op jit(solution)/shard_map/ppermute | solution.py:18
  133.6 27.9 %collective-permute-start.25 = (bf16[1,136,2048]{2,1,0:T(8,128)(2,1)}, bf16[1,136,2048]{2,1,0:T(8,128)(2,1)}, u32[]{:S(2)}, u32[]{:S(2)}) collective-permute-start(bf16[1,136,2048]{2,1,0:T(8,128)(2,1)} %collective-permute-done.24), channel_id=1, source_target_pairs={{0,4},{4,0},{8,12},{12,8},{1,5},{5,1},{9,13},{13,9},{2,6},{6,2},{1... | collective-permute-start | bytes 1671176 | tf_op jit(solution)/shard_map/ppermute | solution.py:18
  159.9 36.1 %collective-permute-start.17 = (bf16[2,136,768]{2,1,0:T(8,128)(2,1)}, bf16[2,136,768]{2,1,0:T(8,128)(2,1)S(1)}, u32[]{:S(2)}, u32[]{:S(2)}) collective-permute-start(bf16[2,136,768]{2,1,0:T(8,128)(2,1)} %constant_dynamic-slice_fusion.1), channel_id=1, source_target_pairs={{0,16},{16,0},{1,17},{17,1},{2,18},{18,2},{3,19},{19,3},{4,20},{20... | collective-permute-start | bytes 1253384 | tf_op jit(solution)/shard_map/ppermute | solution.py:18
  164.8 17.1 %copy-start.3 = (bf16[544,1536]{1,0:T(8,128)(2,1)S(1)}, bf16[544,1536]{1,0:T(8,128)(2,1)}, u32[]{:S(2)}) copy-start(bf16[544,1536]{1,0:T(8,128)(2,1)} %copy-done.2) | copy-start | bytes 5013508
  181.4 23.5 %collective-permute-start.26 = (bf16[2,136,768]{2,1,0:T(8,128)(2,1)}, bf16[2,136,768]{2,1,0:T(8,128)(2,1)}, u32[]{:S(2)}, u32[]{:S(2)}) collective-permute-start(bf16[2,136,768]{2,1,0:T(8,128)(2,1)} %constant_dynamic-slice_fusion), channel_id=1, source_target_pairs={{0,16},{16,0},{1,17},{17,1},{2,18},{18,2},{3,19},{19,3},{4,20},{20... | collective-permute-start | bytes 1253384 | tf_op jit(solution)/shard_map/ppermute | solution.py:18
  196.7 10.6 %collective-permute-start.20 = (bf16[72,768]{1,0:T(8,128)(2,1)S(1)}, bf16[72,768]{1,0:T(8,128)(2,1)S(1)}, u32[]{:S(2)}, u32[]{:S(2)}) collective-permute-start(bf16[72,768]{1,0:T(8,128)(2,1)S(1)} %get-tuple-element.41), channel_id=1, source_target_pairs={{0,1},{1,2},{2,3},{3,0},{4,5},{5,6},{6,7},{7,4},{8,9},{9,10},{10,1... | collective-permute-start | bytes 331784 | tf_op jit(solution)/shard_map/ppermute | solution.py:78
  200.4 10.1 %collective-permute-start.19 = (bf16[72,768]{1,0:T(8,128)(2,1)S(1)}, bf16[72,768]{1,0:T(8,128)(2,1)S(1)}, u32[]{:S(2)}, u32[]{:S(2)}) collective-permute-start(bf16[72,768]{1,0:T(8,128)(2,1)S(1)} %get-tuple-element.42), channel_id=1, source_target_pairs={{0,2},{1,3},{2,0},{3,1},{4,6},{5,7},{6,4},{7,5},{8,10},{9,11},{10,... | collective-permute-start | bytes 331784 | tf_op jit(solution)/shard_map/ppermute | solution.py:78
  202.6 7.9 %collective-permute-start.18 = (bf16[72,768]{1,0:T(8,128)(2,1)S(1)}, bf16[72,768]{1,0:T(8,128)(2,1)S(1)}, u32[]{:S(2)}, u32[]{:S(2)}) collective-permute-start(bf16[72,768]{1,0:T(8,128)(2,1)S(1)} %get-tuple-element.43), channel_id=1, source_target_pairs={{0,3},{1,0},{2,1},{3,2},{4,7},{5,4},{6,5},{7,6},{8,11},{9,8},{10,9... | collective-permute-start | bytes 331784 | tf_op jit(solution)/shard_map/ppermute | solution.py:78
  206.5 14.0 %copy-start.1 = (bf16[128,1536]{1,0:T(8,128)(2,1)S(1)}, bf16[128,1536]{1,0:T(8,128)(2,1)}, u32[]{:S(2)}) copy-start(bf16[128,1536]{1,0:T(8,128)(2,1)} %param.11) | copy-start | bytes 1179652
  206.6 7.8 %collective-permute-start.29 = (bf16[72,768]{1,0:T(8,128)(2,1)S(1)}, bf16[72,768]{1,0:T(8,128)(2,1)S(1)}, u32[]{:S(2)}, u32[]{:S(2)}) collective-permute-start(bf16[72,768]{1,0:T(8,128)(2,1)S(1)} %get-tuple-element.37), channel_id=1, source_target_pairs={{0,1},{1,2},{2,3},{3,0},{4,5},{5,6},{6,7},{7,4},{8,9},{9,10},{10,1... | collective-permute-start | bytes 331784 | tf_op jit(solution)/shard_map/ppermute | solution.py:78
  206.6 12.9 %collective-permute-start.28 = (bf16[72,768]{1,0:T(8,128)(2,1)S(1)}, bf16[72,768]{1,0:T(8,128)(2,1)S(1)}, u32[]{:S(2)}, u32[]{:S(2)}) collective-permute-start(bf16[72,768]{1,0:T(8,128)(2,1)S(1)} %get-tuple-element.38), channel_id=1, source_target_pairs={{0,2},{1,3},{2,0},{3,1},{4,6},{5,7},{6,4},{7,5},{8,10},{9,11},{10,... | collective-permute-start | bytes 331784 | tf_op jit(solution)/shard_map/ppermute | solution.py:78
  207.2 12.3 %collective-permute-start.27 = (bf16[72,768]{1,0:T(8,128)(2,1)S(1)}, bf16[72,768]{1,0:T(8,128)(2,1)S(1)}, u32[]{:S(2)}, u32[]{:S(2)}) collective-permute-start(bf16[72,768]{1,0:T(8,128)(2,1)S(1)} %get-tuple-element.39), channel_id=1, source_target_pairs={{0,3},{1,0},{2,1},{3,2},{4,7},{5,4},{6,5},{7,6},{8,11},{9,8},{10,9... | collective-permute-start | bytes 331784 | tf_op jit(solution)/shard_map/ppermute | solution.py:78
  (10 other events, 58.3 us)

commit v3 on v2

--- a/solution.py
+++ b/solution.py
@@ -47,13 +47,18 @@
     return first, second
 
 
-def share_of_features(value, pairs):
+def across(value, pairs):
+    if lax.axis_size("dp") != 4 or pairs % 4:
+        return value
+    return swap(value, "dp", 2)
+
+
+def share_of_features(value, far, pairs):
     if lax.axis_size("dp") != 4 or pairs % 4:
         return lax.all_gather(value, "dp", axis=2, tiled=True)
     me = lax.axis_index("dp")
     core, chip = me % 2, me // 2
     near = swap(value, "dp", 1)
-    far = swap(value, "dp", 2)
     far_near = swap(far, "dp", 1)
     low, high = in_order(value, near, core)
     far_low, far_high = in_order(far, far_near, core)
@@ -85,11 +90,14 @@
     return jnp.concatenate(in_order(value, other, lax.axis_index("pipe")), axis=1)
 
 
-def deliver(chunks):
+def send_out(chunks):
     groups = lax.axis_size("expert")
     width = chunks.shape[2] // lax.axis_size("pipe")
     start = lax.axis_index("pipe") * width
-    moved = [shifted(lax.dynamic_slice_in_dim(chunks[s], start, width, 1), s) for s in range(1, groups)]
+    return [shifted(lax.dynamic_slice_in_dim(chunks[s], start, width, 1), s) for s in range(1, groups)]
+
+
+def in_full(chunks, moved):
     return jnp.concatenate([chunks[0]] + [all_features(part) for part in moved], axis=0)
 
 
@@ -132,18 +140,21 @@
         placed = jnp.dot(order, arrivals, preferred_element_type=F32).astype(BF)
         return placed.reshape(pairs, rows, features)
 
-    arrivals = deliver(spread(tokens).astype(BF))
-    grad_arrivals = deliver((spread(cotangent) * slot_weight[:, :, None]).astype(BF))
-    arrived = by_pair(arrivals)
+    chunks = spread(tokens).astype(BF)
+    moved, late_cotangent = lax.optimization_barrier((send_out(chunks), cotangent))
+    grad_chunks = (spread(late_cotangent) * slot_weight[:, :, None]).astype(BF)
+    grad_moved = send_out(grad_chunks)
+    arrived = by_pair(in_full(chunks, moved))
     pre_part = jnp.einsum("pcd,pdh->pch", arrived, w_up, preferred_element_type=F32).astype(BF)
-    pre_near = near_sum(pre_part)
-    grad_rows, pre_near = lax.optimization_barrier((by_pair(grad_arrivals), pre_near))
+    pre_part, grad_arrivals = lax.optimization_barrier((pre_part, in_full(grad_chunks, grad_moved)))
+    grad_rows, pre_near = lax.optimization_barrier((by_pair(grad_arrivals), near_sum(pre_part)))
     pre_share = far_sum(pre_near)
     grad_part = jnp.einsum("pcd,phd->pch", grad_rows, w_down, preferred_element_type=F32).astype(BF)
-
-    hidden = share_of_features(jax.nn.silu(pre_share).astype(BF), pairs)
-    grad_share = far_sum(near_sum(grad_part))
-    grad_pre = share_of_features((grad_share * silu_slope(pre_share)).astype(BF), pairs)
+    hidden_share = jax.nn.silu(pre_share).astype(BF)
+    grad_part, pre_share, hidden_share = lax.optimization_barrier((grad_part, pre_share, hidden_share))
+    grad_near, hidden_far = lax.optimization_barrier((near_sum(grad_part), across(hidden_share, pairs)))
+    hidden = share_of_features(hidden_share, hidden_far, pairs)
+    grad_share = far_sum(grad_near)
 
     def by_set(value):
         return value.reshape((sets, halves) + value.shape[1:])
@@ -156,21 +167,29 @@
         return jnp.concatenate(moved, axis=0)
 
     out_part = jnp.einsum("rhck,rhkd->rcd", by_set(hidden), by_set(w_down), preferred_element_type=F32)
-    out_home = back_to_tokens(sum_over_hidden(out_part))
+    out_part, late_hidden, grad_share = lax.optimization_barrier((out_part.astype(BF), hidden, grad_share))
+    grad_pre_share = (grad_share * silu_slope(pre_share)).astype(BF)
+    grad_pre = share_of_features(grad_pre_share, across(grad_pre_share, pairs), pairs)
+    down_grad = jnp.einsum("pch,pcd->phd", late_hidden, grad_rows, preferred_element_type=F32).astype(BF)
+    grad_pre, down_grad, out_rows = lax.optimization_barrier(
+        (grad_pre, down_grad, sum_over_hidden(out_part))
+    )
+    out_home = back_to_tokens(out_rows)
+    back_part = jnp.einsum("rhck,rhdk->rcd", by_set(grad_pre), by_set(w_up), preferred_element_type=F32)
+    back_part, late_grad_pre, out_home = lax.optimization_barrier(
+        (back_part.astype(BF), grad_pre, out_home)
+    )
+    up_grad = jnp.einsum("pcd,pch->pdh", arrived, late_grad_pre, preferred_element_type=F32).astype(BF)
     output = lax.dot_general(
         weighting.reshape(groups * slots, own), out_home.astype(F32),
         (((0,), (0,)), ((), ())), precision=lax.Precision.HIGHEST,
     ).astype(BF)
-    down_grad = jnp.einsum("pch,pcd->phd", hidden, grad_rows, preferred_element_type=F32).astype(BF)
-    grad_pre, down_grad = lax.optimization_barrier((grad_pre, down_grad))
-    back_part = jnp.einsum("rhck,rhdk->rcd", by_set(grad_pre), by_set(w_up), preferred_element_type=F32)
-    back_part, late = lax.optimization_barrier((back_part.astype(BF), grad_pre))
-    back_home = back_to_tokens(sum_over_hidden(back_part))
+    back_rows, up_grad, output = lax.optimization_barrier((sum_over_hidden(back_part), up_grad, output))
+    back_home = back_to_tokens(back_rows)
     token_grad = lax.dot_general(
         routing.reshape(groups * slots, own), back_home, (((0,), (0,)), ((), ())),
         preferred_element_type=F32,
     ).astype(BF)
-    up_grad = jnp.einsum("pcd,pch->pdh", arrived, late, preferred_element_type=F32).astype(BF)
     return (output, token_grad, up_grad, down_grad)
 
 

time: 221 us -> 187 us (0.85)
  waiting for transfers between devices: 72.5 us -> 44 us
  local copies, waits for them, and re-layouts: 11 us -> 6.8 us
    ppermute x18, waiting for transfers between devices: 57.1 us -> 30.2 us  [swap(): return lax.ppermute(value, axis, [(i, i ^ bit) for i in range(count)])]
    add x0 -> x3, other arithmetic: none -> 2.34 us  [the longest x2 2.21 us: sum_over_hidden(): lax.dynamic_slice_in_dim(part, me * width, width, 2).astype(F32)]
  transfers between devices with their start and end apart: 30 -> 30, of which waited for: 12 -> 12; matrix products, arithmetic and copies ran while one was open for 38% -> 47% of each run, Pallas kernels for 0% -> 0%
where the time goes in v3:
time: 187 us
  matrix products  84.4 us (45%)
  waiting for transfers between devices  44 us (24%)
  starting transfers between devices  35.9 us (19%)
  other arithmetic  14.7 us (8%)
  local copies, waits for them, and re-layouts  6.8 us (4%)
    ppermute x18, waiting for transfers between devices, swap(): return lax.ppermute(value, axis, [(i, i ^ bit) for i in range(count)])  30.2 us
    ppermute x12, starting transfers between devices, shifted(): lax.ppermute(value, 'expert', [(i, (i + by) % count) for i in range(count)])  21.9 us
    dot_general x1, matrix products, on_device(): jnp.einsum('pcd,pch->pdh', arrived, late_grad_pre, preferred_element_type...  14.1 us
    ppermute x18, starting transfers between devices, swap(): return lax.ppermute(value, axis, [(i, i ^ bit) for i in range(count)])  14 us
    dot_general x1, matrix products, on_device(): jnp.einsum('pch,pcd->phd', late_hidden, grad_rows, preferred_element_type...  13.9 us
    ppermute x12, waiting for transfers between devices, shifted(): lax.ppermute(value, 'expert', [(i, (i + by) % count) for i in range(count)])  13.8 us
    dot_general x1, matrix products, on_device(): jnp.einsum('pcd,phd->pch', grad_rows, w_down, preferred_element_type=F32)  13.6 us
    dot_general x1, matrix products, on_device(): jnp.einsum('rhck,rhdk->rcd', by_set(grad_pre), by_set(w_up), preferred_el...  13.2 us
  transfers between devices with their start and end apart: 30, of which 12 were waited for; matrix products, arithmetic and copies ran while one was open for 47% of the time, Pallas kernels for 0%

profile of v3, /device:TPU:0, one launch (start us, length us, event | category | flops | bytes accessed | tf_op | source)
XLA Modules:
  0.0 186.9 jit_solution(11936529728142684817)
XLA Ops:
  2.2 3.1 %collective-permute-start = (bf16[72,768]{1,0:T(8,128)(2,1)S(1)}, bf16[72,768]{1,0:T(8,128)(2,1)S(1)}, u32[]{:S(2)}, u32[]{:S(2)}) collective-permute-start(bf16[72,768]{1,0:T(8,128)(2,1)S(1)} %dynamic-slice_bitcast_fusion.9), channel_id=1, source_target_pairs={{0,1},{1,2},{2,3},{3,0},{4,5},{5,6},{6,7},{7,4},{8,9},{9,10},{10,1... | collective-permute-start | bytes 331784 | tf_op jit(solution)/shard_map/ppermute | solution.py:83
  5.3 2.7 %collective-permute-start.1 = (bf16[72,768]{1,0:T(8,128)(2,1)S(1)}, bf16[72,768]{1,0:T(8,128)(2,1)S(1)}, u32[]{:S(2)}, u32[]{:S(2)}) collective-permute-start(bf16[72,768]{1,0:T(8,128)(2,1)S(1)} %dynamic-slice_bitcast_fusion.8), channel_id=1, source_target_pairs={{0,2},{1,3},{2,0},{3,1},{4,6},{5,7},{6,4},{7,5},{8,10},{9,11},{10,... | collective-permute-start | bytes 331784 | tf_op jit(solution)/shard_map/ppermute | solution.py:83
  7.9 1.4 collective-permute-start.2
  9.7 1.6 collective-permute-done
  11.3 3.9 %collective-permute-done.1 = bf16[72,768]{1,0:T(8,128)(2,1)S(1)} collective-permute-done((bf16[72,768]{1,0:T(8,128)(2,1)S(1)}, bf16[72,768]{1,0:T(8,128)(2,1)S(1)}, u32[]{:S(2)}, u32[]{:S(2)}) %collective-permute-start.1) | collective-permute-done | bytes 110624 | tf_op jit(solution)/shard_map/ppermute | solution.py:83
  15.2 1.5 collective-permute-start.3
  17.3 1.5 collective-permute-start.5
  19.3 2.8 %collective-permute-start.6 = (bf16[72,768]{1,0:T(8,128)(2,1)S(1)}, bf16[72,768]{1,0:T(8,128)(2,1)S(1)}, u32[]{:S(2)}, u32[]{:S(2)}) collective-permute-start(bf16[72,768]{1,0:T(8,128)(2,1)S(1)} %dynamic-slice_bitcast_fusion.6), channel_id=1, source_target_pairs={{0,1},{1,2},{2,3},{3,0},{4,5},{5,6},{6,7},{7,4},{8,9},{9,10},{10,1... | collective-permute-start | bytes 331784 | tf_op jit(solution)/shard_map/ppermute | solution.py:83
  22.2 1.6 collective-permute-start.8
  27.9 11.8 %convolution_convert_fusion.4 = bf16[4,136,2048]{2,1,0:T(8,128)(2,1)S(1)} fusion(bf16[4,136,1536]{2,1,0:T(8,128)(2,1)S(1)} %bitcast.105, bf16[4,1536,2048]{2,1,0:T(8,128)(2,1)} %param.9), kind=kOutput, calls=%fused_computation.4 | convolution fusion | flops 3423666176 | bytes 29065216 | tf_op jit(solution)/shard_map/pcd,pdh->pch/dot_general | solution.py:148
  41.8 2.7 %collective-permute-done.9 = bf16[72,768]{1,0:T(8,128)(2,1)S(1)} collective-permute-done((bf16[72,768]{1,0:T(8,128)(2,1)S(1)}, bf16[72,768]{1,0:T(8,128)(2,1)S(1)}, u32[]{:S(2)}, u32[]{:S(2)}) %collective-permute-start.9) | collective-permute-done | bytes 110624 | tf_op jit(solution)/shard_map/ppermute | solution.py:18
  46.9 2.3 %convolution_convert_fusion.3 = bf16[544,1536]{1,0:T(8,128)(2,1)} fusion(bf16[288,1536]{1,0:T(8,128)(2,1)S(1)} %maximum_maximum_fusion, s32[544]{0:T(1024)S(1)} %fusion.35), kind=kOutput, calls=%fused_computation.3 | convolution fusion | flops 482288640 | bytes 2558080 | tf_op jit(solution)/shard_map/dot_general | solution.py:140
  50.0 1.7 fusion.4
  52.6 1.5 collective-permute-start.13
  54.1 13.6 %convolution_convert_fusion.2 = bf16[4,136,2048]{2,1,0:T(8,128)(2,1)S(1)} fusion(bf16[4,136,1536]{2,1,0:T(8,128)(2,1)} %bitcast.111, bf16[4,2048,1536]{2,1,0:T(8,128)(2,1)} %param.10), kind=kOutput, calls=%fused_computation.2 | convolution fusion | flops 3423666176 | bytes 29065216 | tf_op jit(solution)/shard_map/pcd,phd->pch/dot_general | solution.py:152
  67.8 2.5 %multiply_convert_fusion.1 = (bf16[1,136,2048]{2,1,0:T(8,128)(2,1)S(1)}, f32[1,136,2048]{2,1,0:T(8,128)}) fusion(bf16[1,136,2048]{2,1,0:T(8,128)(2,1)} %collective-permute-done.13, bf16[2,1,136,2048]{3,2,1,0:T(8,128)(2,1)} %copy-done.7, s32[]{:T(128)S(6)} %select_n.279), kind=kLoop, calls=%fused_computation.27 | loop fusion | flops 2228224 | bytes 2785284 | tf_op jit(solution)/shard_map/convert_element_type | solution.py:153
  73.2 1.4 fusion.3
  74.6 11.0 %collective-permute-done.16 = bf16[1,136,2048]{2,1,0:T(8,128)(2,1)} collective-permute-done((bf16[1,136,2048]{2,1,0:T(8,128)(2,1)S(1)}, bf16[1,136,2048]{2,1,0:T(8,128)(2,1)}, u32[]{:S(2)}, u32[]{:S(2)}) %collective-permute-start.16) | collective-permute-done | bytes 557088 | tf_op jit(solution)/shard_map/ppermute | solution.py:18
  87.9 1.4 broadcast_select_fusion.15
  89.6 10.3 %fusion.1 = bf16[2,136,1536]{2,1,0:T(8,128)(2,1)S(1)} fusion(bf16[2,2,136,2048]{3,2,1,0:T(8,128)(2,1)S(1)} %bitcast.107, bf16[2,2,2048,1536]{3,2,1,0:T(8,128)(2,1)} %bitcast.101), kind=kOutput, calls=%fused_computation.11 | convolution fusion | flops 3422969856 | bytes 28229632 | tf_op jit(solution)/shard_map/rhck,rhkd->rcd/dot_general | solution.py:169
  99.9 1.9 %collective-permute-done.18 = bf16[1,136,2048]{2,1,0:T(8,128)(2,1)S(1)} collective-permute-done((bf16[1,136,2048]{2,1,0:T(8,128)(2,1)S(1)}, bf16[1,136,2048]{2,1,0:T(8,128)(2,1)S(1)}, u32[]{:S(2)}, u32[]{:S(2)}) %collective-permute-start.18) | collective-permute-done | bytes 557088 | tf_op jit(solution)/shard_map/ppermute | solution.py:18
  106.6 11.2 %collective-permute-done.20 = bf16[1,136,2048]{2,1,0:T(8,128)(2,1)} collective-permute-done((bf16[1,136,2048]{2,1,0:T(8,128)(2,1)}, bf16[1,136,2048]{2,1,0:T(8,128)(2,1)}, u32[]{:S(2)}, u32[]{:S(2)}) %collective-permute-start.20) | collective-permute-done | bytes 557088 | tf_op jit(solution)/shard_map/ppermute | solution.py:18
  117.8 13.9 %convolution_convert_fusion.1 = bf16[4,2048,1536]{2,1,0:T(8,128)(2,1)} fusion(bf16[4,136,2048]{2,1,0:T(8,128)(2,1)S(1)} %pad_maximum_fusion, bf16[4,136,1536]{2,1,0:T(8,128)(2,1)} %bitcast.112), kind=kOutput, calls=%fused_computation.1 | convolution fusion | flops 3435134976 | bytes 29065216 | tf_op jit(solution)/shard_map/pch,pcd->phd/dot_general | solution.py:173
  132.8 1.7 broadcast_select_fusion.11
  136.2 2.9 %collective-permute-start.25 = (bf16[72,768]{1,0:T(8,128)(2,1)}, bf16[72,768]{1,0:T(8,128)(2,1)}, u32[]{:S(2)}, u32[]{:S(2)}) collective-permute-start(bf16[72,768]{1,0:T(8,128)(2,1)} %get-tuple-element.79), channel_id=1, source_target_pairs={{0,1},{1,2},{2,3},{3,0},{4,5},{5,6},{6,7},{7,4},{8,9},{9,10},{10,1... | collective-permute-start | bytes 331784 | tf_op jit(solution)/shard_map/ppermute | solution.py:83
  139.4 2.1 %collective-permute-start.23 = (bf16[72,768]{1,0:T(8,128)(2,1)S(1)}, bf16[72,768]{1,0:T(8,128)(2,1)}, u32[]{:S(2)}, u32[]{:S(2)}) collective-permute-start(bf16[72,768]{1,0:T(8,128)(2,1)S(1)} %get-tuple-element.81), channel_id=1, source_target_pairs={{0,3},{1,0},{2,1},{3,2},{4,7},{5,4},{6,5},{7,6},{8,11},{9,8},{10,9... | collective-permute-start | bytes 331784 | tf_op jit(solution)/shard_map/ppermute | solution.py:83
  141.5 13.2 %fusion.2 = bf16[2,136,1536]{2,1,0:T(8,128)(2,1)S(1)} fusion(bf16[2,2,136,2048]{3,2,1,0:T(8,128)(2,1)S(1)} %bitcast.108, bf16[2,2,1536,2048]{3,2,1,0:T(8,128)(2,1)} %bitcast.102), kind=kOutput, calls=%fused_computation.12 | convolution fusion | flops 3422969856 | bytes 28229632 | tf_op jit(solution)/shard_map/rhck,rhdk->rcd/dot_general | solution.py:178
  157.7 14.1 %convolution_convert_fusion = bf16[4,1536,2048]{2,1,0:T(8,128)(2,1)} fusion(bf16[4,136,1536]{2,1,0:T(8,128)(2,1)S(1)} %bitcast.106, bf16[4,136,2048]{2,1,0:T(8,128)(2,1)} %copy-done.4), kind=kOutput, calls=%fused_computation | convolution fusion | flops 3435134976 | bytes 29065216 | tf_op jit(solution)/shard_map/pcd,pch->pdh/dot_general | solution.py:182
  174.7 2.4 %collective-permute-start.28 = (bf16[72,768]{1,0:T(8,128)(2,1)S(1)}, bf16[72,768]{1,0:T(8,128)(2,1)S(1)}, u32[]{:S(2)}, u32[]{:S(2)}) collective-permute-start(bf16[72,768]{1,0:T(8,128)(2,1)S(1)} %get-tuple-element.76), channel_id=1, source_target_pairs={{0,2},{1,3},{2,0},{3,1},{4,6},{5,7},{6,4},{7,5},{8,10},{9,11},{10,... | collective-permute-start | bytes 331784 | tf_op jit(solution)/shard_map/ppermute | solution.py:83
  177.1 1.4 collective-permute-start.27
  178.5 4.0 %collective-permute-done.29 = bf16[72,768]{1,0:T(8,128)(2,1)S(1)} collective-permute-done((bf16[72,768]{1,0:T(8,128)(2,1)S(1)}, bf16[72,768]{1,0:T(8,128)(2,1)S(1)}, u32[]{:S(2)}, u32[]{:S(2)}) %collective-permute-start.29) | collective-permute-done | bytes 110624 | tf_op jit(solution)/shard_map/ppermute | solution.py:83
  182.5 3.3 %collective-permute-done.28 = bf16[72,768]{1,0:T(8,128)(2,1)S(1)} collective-permute-done((bf16[72,768]{1,0:T(8,128)(2,1)S(1)}, bf16[72,768]{1,0:T(8,128)(2,1)S(1)}, u32[]{:S(2)}, u32[]{:S(2)}) %collective-permute-start.28) | collective-permute-done | bytes 110624 | tf_op jit(solution)/shard_map/ppermute | solution.py:83
  (113 shorter events, 33.2 us)
Async XLA Ops:
  1.7 17.1 %copy-start.8 = (bf16[128,1536]{1,0:T(8,128)(2,1)S(1)}, bf16[128,1536]{1,0:T(8,128)(2,1)}, u32[]{:S(2)}) copy-start(bf16[128,1536]{1,0:T(8,128)(2,1)} %param.11) | copy-start | bytes 1179652
  2.2 9.1 %collective-permute-start = (bf16[72,768]{1,0:T(8,128)(2,1)S(1)}, bf16[72,768]{1,0:T(8,128)(2,1)S(1)}, u32[]{:S(2)}, u32[]{:S(2)}) collective-permute-start(bf16[72,768]{1,0:T(8,128)(2,1)S(1)} %dynamic-slice_bitcast_fusion.9), channel_id=1, source_target_pairs={{0,1},{1,2},{2,3},{3,0},{4,5},{5,6},{6,7},{7,4},{8,9},{9,10},{10,1... | collective-permute-start | bytes 331784 | tf_op jit(solution)/shard_map/ppermute | solution.py:83
  5.3 9.9 %collective-permute-start.1 = (bf16[72,768]{1,0:T(8,128)(2,1)S(1)}, bf16[72,768]{1,0:T(8,128)(2,1)S(1)}, u32[]{:S(2)}, u32[]{:S(2)}) collective-permute-start(bf16[72,768]{1,0:T(8,128)(2,1)S(1)} %dynamic-slice_bitcast_fusion.8), channel_id=1, source_target_pairs={{0,2},{1,3},{2,0},{3,1},{4,6},{5,7},{6,4},{7,5},{8,10},{9,11},{10,... | collective-permute-start | bytes 331784 | tf_op jit(solution)/shard_map/ppermute | solution.py:83
  7.9 7.3 %collective-permute-start.2 = (bf16[72,768]{1,0:T(8,128)(2,1)S(1)}, bf16[72,768]{1,0:T(8,128)(2,1)S(1)}, u32[]{:S(2)}, u32[]{:S(2)}) collective-permute-start(bf16[72,768]{1,0:T(8,128)(2,1)S(1)} %dynamic-slice_bitcast_fusion.7), channel_id=1, source_target_pairs={{0,3},{1,0},{2,1},{3,2},{4,7},{5,4},{6,5},{7,6},{8,11},{9,8},{10,9... | collective-permute-start | bytes 331784 | tf_op jit(solution)/shard_map/ppermute | solution.py:83
  15.2 8.5 %collective-permute-start.3 = (bf16[72,768]{1,0:T(8,128)(2,1)S(1)}, bf16[72,768]{1,0:T(8,128)(2,1)S(1)}, u32[]{:S(2)}, u32[]{:S(2)}) collective-permute-start(bf16[72,768]{1,0:T(8,128)(2,1)S(1)} %collective-permute-done), channel_id=1, source_target_pairs={{0,16},{16,0},{1,17},{17,1},{2,18},{18,2},{3,19},{19,3},{4,20},{20... | collective-permute-start | bytes 331784 | tf_op jit(solution)/shard_map/ppermute | solution.py:18
  16.8 8.2 %collective-permute-start.4 = (bf16[72,768]{1,0:T(8,128)(2,1)S(1)}, bf16[72,768]{1,0:T(8,128)(2,1)S(1)}, u32[]{:S(2)}, u32[]{:S(2)}) collective-permute-start(bf16[72,768]{1,0:T(8,128)(2,1)S(1)} %collective-permute-done.1), channel_id=1, source_target_pairs={{0,16},{16,0},{1,17},{17,1},{2,18},{18,2},{3,19},{19,3},{4,20},{20... | collective-permute-start | bytes 331784 | tf_op jit(solution)/shard_map/ppermute | solution.py:18
  17.3 7.8 %collective-permute-start.5 = (bf16[72,768]{1,0:T(8,128)(2,1)S(1)}, bf16[72,768]{1,0:T(8,128)(2,1)S(1)}, u32[]{:S(2)}, u32[]{:S(2)}) collective-permute-start(bf16[72,768]{1,0:T(8,128)(2,1)S(1)} %collective-permute-done.2), channel_id=1, source_target_pairs={{0,16},{16,0},{1,17},{17,1},{2,18},{18,2},{3,19},{19,3},{4,20},{20... | collective-permute-start | bytes 331784 | tf_op jit(solution)/shard_map/ppermute | solution.py:18
  19.3 7.7 %collective-permute-start.6 = (bf16[72,768]{1,0:T(8,128)(2,1)S(1)}, bf16[72,768]{1,0:T(8,128)(2,1)S(1)}, u32[]{:S(2)}, u32[]{:S(2)}) collective-permute-start(bf16[72,768]{1,0:T(8,128)(2,1)S(1)} %dynamic-slice_bitcast_fusion.6), channel_id=1, source_target_pairs={{0,1},{1,2},{2,3},{3,0},{4,5},{5,6},{6,7},{7,4},{8,9},{9,10},{10,1... | collective-permute-start | bytes 331784 | tf_op jit(solution)/shard_map/ppermute | solution.py:83
  22.2 17.5 %collective-permute-start.8 = (bf16[72,768]{1,0:T(8,128)(2,1)S(1)}, bf16[72,768]{1,0:T(8,128)(2,1)S(1)}, u32[]{:S(2)}, u32[]{:S(2)}) collective-permute-start(bf16[72,768]{1,0:T(8,128)(2,1)S(1)} %dynamic-slice_bitcast_fusion.5), channel_id=1, source_target_pairs={{0,2},{1,3},{2,0},{3,1},{4,6},{5,7},{6,4},{7,5},{8,10},{9,11},{10,... | collective-permute-start | bytes 331784 | tf_op jit(solution)/shard_map/ppermute | solution.py:83
  23.8 17.2 %collective-permute-start.10 = (bf16[72,768]{1,0:T(8,128)(2,1)S(1)}, bf16[72,768]{1,0:T(8,128)(2,1)S(1)}, u32[]{:S(2)}, u32[]{:S(2)}) collective-permute-start(bf16[72,768]{1,0:T(8,128)(2,1)S(1)} %dynamic-slice_bitcast_fusion.4), channel_id=1, source_target_pairs={{0,3},{1,0},{2,1},{3,2},{4,7},{5,4},{6,5},{7,6},{8,11},{9,8},{10,9... | collective-permute-start | bytes 331784 | tf_op jit(solution)/shard_map/ppermute | solution.py:83
  27.1 14.7 %collective-permute-start.7 = (bf16[72,768]{1,0:T(8,128)(2,1)S(1)}, bf16[72,768]{1,0:T(8,128)(2,1)S(1)}, u32[]{:S(2)}, u32[]{:S(2)}) collective-permute-start(bf16[72,768]{1,0:T(8,128)(2,1)S(1)} %collective-permute-done.6), channel_id=1, source_target_pairs={{0,16},{16,0},{1,17},{17,1},{2,18},{18,2},{3,19},{19,3},{4,20},{20... | collective-permute-start | bytes 331784 | tf_op jit(solution)/shard_map/ppermute | solution.py:18
  39.7 4.8 %collective-permute-start.9 = (bf16[72,768]{1,0:T(8,128)(2,1)S(1)}, bf16[72,768]{1,0:T(8,128)(2,1)S(1)}, u32[]{:S(2)}, u32[]{:S(2)}) collective-permute-start(bf16[72,768]{1,0:T(8,128)(2,1)S(1)} %collective-permute-done.8), channel_id=1, source_target_pairs={{0,16},{16,0},{1,17},{17,1},{2,18},{18,2},{3,19},{19,3},{4,20},{20... | collective-permute-start | bytes 331784 | tf_op jit(solution)/shard_map/ppermute | solution.py:18
  41.0 4.7 %collective-permute-start.11 = (bf16[72,768]{1,0:T(8,128)(2,1)S(1)}, bf16[72,768]{1,0:T(8,128)(2,1)S(1)}, u32[]{:S(2)}, u32[]{:S(2)}) collective-permute-start(bf16[72,768]{1,0:T(8,128)(2,1)S(1)} %collective-permute-done.10), channel_id=1, source_target_pairs={{0,16},{16,0},{1,17},{17,1},{2,18},{18,2},{3,19},{19,3},{4,20},{20... | collective-permute-start | bytes 331784 | tf_op jit(solution)/shard_map/ppermute | solution.py:18
  46.9 3.1 %collective-permute-start.12 = (bf16[2,1,136,2048]{3,2,1,0:T(8,128)(2,1)}, bf16[2,1,136,2048]{3,2,1,0:T(8,128)(2,1)}, u32[]{:S(2)}, u32[]{:S(2)}) collective-permute-start(bf16[2,1,136,2048]{3,2,1,0:T(8,128)(2,1)} %dynamic-slice_bitcast_fusion.1), channel_id=1, source_target_pairs={{0,4},{4,0},{8,12},{12,8},{1,5},{5,1},{9,13},{13,9},{2,6},{6,2},{1... | collective-permute-start | bytes 3342344 | tf_op jit(solution)/shard_map/ppermute | solution.py:18
  52.6 15.1 %collective-permute-start.13 = (bf16[1,136,2048]{2,1,0:T(8,128)(2,1)S(1)}, bf16[1,136,2048]{2,1,0:T(8,128)(2,1)}, u32[]{:S(2)}, u32[]{:S(2)}) collective-permute-start(bf16[1,136,2048]{2,1,0:T(8,128)(2,1)S(1)} %dynamic-slice_bitcast_fusion.3), channel_id=1, source_target_pairs={{0,8},{4,12},{8,0},{12,4},{1,9},{5,13},{9,1},{13,5},{2,10},{6,14},... | collective-permute-start | bytes 1671176 | tf_op jit(solution)/shard_map/ppermute | solution.py:18
  70.4 2.8 %collective-permute-start.15 = (bf16[2,1,136,2048]{3,2,1,0:T(8,128)(2,1)S(1)}, bf16[2,1,136,2048]{3,2,1,0:T(8,128)(2,1)S(1)}, u32[]{:S(2)}, u32[]{:S(2)}) collective-permute-start(bf16[2,1,136,2048]{3,2,1,0:T(8,128)(2,1)S(1)} %dynamic-slice_bitcast_fusion), channel_id=1, source_target_pairs={{0,4},{4,0},{8,12},{12,8},{1,5},{5,1},{9,13},{13,9},{2,6},{6,2},{1... | collective-permute-start | bytes 3342344 | tf_op jit(solution)/shard_map/ppermute | solution.py:18
  70.5 15.1 %collective-permute-start.16 = (bf16[1,136,2048]{2,1,0:T(8,128)(2,1)S(1)}, bf16[1,136,2048]{2,1,0:T(8,128)(2,1)}, u32[]{:S(2)}, u32[]{:S(2)}) collective-permute-start(bf16[1,136,2048]{2,1,0:T(8,128)(2,1)S(1)} %get-tuple-element.37), channel_id=1, source_target_pairs={{0,8},{4,12},{8,0},{12,4},{1,9},{5,13},{9,1},{13,5},{2,10},{6,14},... | collective-permute-start | bytes 1671176 | tf_op jit(solution)/shard_map/ppermute | solution.py:18
  71.7 16.2 %collective-permute-start.14 = (bf16[1,136,2048]{2,1,0:T(8,128)(2,1)S(1)}, bf16[1,136,2048]{2,1,0:T(8,128)(2,1)}, u32[]{:S(2)}, u32[]{:S(2)}) collective-permute-start(bf16[1,136,2048]{2,1,0:T(8,128)(2,1)S(1)} %get-tuple-element.37), channel_id=1, source_target_pairs={{0,4},{4,0},{8,12},{12,8},{1,5},{5,1},{9,13},{13,9},{2,6},{6,2},{1... | collective-permute-start | bytes 1671176 | tf_op jit(solution)/shard_map/ppermute | solution.py:18
  85.6 2.3 %collective-permute-start.17 = (bf16[1,136,2048]{2,1,0:T(8,128)(2,1)}, bf16[1,136,2048]{2,1,0:T(8,128)(2,1)S(1)}, u32[]{:S(2)}, u32[]{:S(2)}) collective-permute-start(bf16[1,136,2048]{2,1,0:T(8,128)(2,1)} %collective-permute-done.16), channel_id=1, source_target_pairs={{0,4},{4,0},{8,12},{12,8},{1,5},{5,1},{9,13},{13,9},{2,6},{6,2},{1... | collective-permute-start | bytes 1671176 | tf_op jit(solution)/shard_map/ppermute | solution.py:18
  86.7 15.1 %collective-permute-start.18 = (bf16[1,136,2048]{2,1,0:T(8,128)(2,1)S(1)}, bf16[1,136,2048]{2,1,0:T(8,128)(2,1)S(1)}, u32[]{:S(2)}, u32[]{:S(2)}) collective-permute-start(bf16[1,136,2048]{2,1,0:T(8,128)(2,1)S(1)} %dynamic-slice_bitcast_fusion.2), channel_id=1, source_target_pairs={{0,8},{4,12},{8,0},{12,4},{1,9},{5,13},{9,1},{13,5},{2,10},{6,14},... | collective-permute-start | bytes 1671176 | tf_op jit(solution)/shard_map/ppermute | solution.py:18
  103.2 14.6 %collective-permute-start.20 = (bf16[1,136,2048]{2,1,0:T(8,128)(2,1)}, bf16[1,136,2048]{2,1,0:T(8,128)(2,1)}, u32[]{:S(2)}, u32[]{:S(2)}) collective-permute-start(bf16[1,136,2048]{2,1,0:T(8,128)(2,1)} %multiply_convert_fusion), channel_id=1, source_target_pairs={{0,8},{4,12},{8,0},{12,4},{1,9},{5,13},{9,1},{13,5},{2,10},{6,14},... | collective-permute-start | bytes 1671176 | tf_op jit(solution)/shard_map/ppermute | solution.py:18
  104.5 30.3 %copy-start.9 = (pred[2,1,136,288]{3,2,1,0:T(8,128)(4,1)}, pred[2,1,136,288]{3,2,1,0:T(8,128)(4,1)S(1)}, u32[]{:S(2)}) copy-start(pred[2,1,136,288]{3,2,1,0:T(8,128)(4,1)S(1)} %iota_compare_fusion.3) | copy-start | bytes 235012
  104.5 28.3 %collective-permute-start.19 = (bf16[1,136,2048]{2,1,0:T(8,128)(2,1)}, bf16[1,136,2048]{2,1,0:T(8,128)(2,1)}, u32[]{:S(2)}, u32[]{:S(2)}) collective-permute-start(bf16[1,136,2048]{2,1,0:T(8,128)(2,1)} %multiply_convert_fusion), channel_id=1, source_target_pairs={{0,4},{4,0},{8,12},{12,8},{1,5},{5,1},{9,13},{13,9},{2,6},{6,2},{1... | collective-permute-start | bytes 1671176 | tf_op jit(solution)/shard_map/ppermute | solution.py:18
  105.4 26.3 %collective-permute-start.22 = (bf16[2,136,768]{2,1,0:T(8,128)(2,1)}, bf16[2,136,768]{2,1,0:T(8,128)(2,1)}, u32[]{:S(2)}, u32[]{:S(2)}) collective-permute-start(bf16[2,136,768]{2,1,0:T(8,128)(2,1)} %constant_dynamic-slice_fusion.1), channel_id=1, source_target_pairs={{0,16},{16,0},{1,17},{17,1},{2,18},{18,2},{3,19},{19,3},{4,20},{20... | collective-permute-start | bytes 1253384 | tf_op jit(solution)/shard_map/ppermute | solution.py:18
  117.8 15.0 %collective-permute-start.21 = (bf16[1,136,2048]{2,1,0:T(8,128)(2,1)}, bf16[1,136,2048]{2,1,0:T(8,128)(2,1)}, u32[]{:S(2)}, u32[]{:S(2)}) collective-permute-start(bf16[1,136,2048]{2,1,0:T(8,128)(2,1)} %collective-permute-done.20), channel_id=1, source_target_pairs={{0,4},{4,0},{8,12},{12,8},{1,5},{5,1},{9,13},{13,9},{2,6},{6,2},{1... | collective-permute-start | bytes 1671176 | tf_op jit(solution)/shard_map/ppermute | solution.py:18
  136.2 18.5 %collective-permute-start.25 = (bf16[72,768]{1,0:T(8,128)(2,1)}, bf16[72,768]{1,0:T(8,128)(2,1)}, u32[]{:S(2)}, u32[]{:S(2)}) collective-permute-start(bf16[72,768]{1,0:T(8,128)(2,1)} %get-tuple-element.79), channel_id=1, source_target_pairs={{0,1},{1,2},{2,3},{3,0},{4,5},{5,6},{6,7},{7,4},{8,9},{9,10},{10,1... | collective-permute-start | bytes 331784 | tf_op jit(solution)/shard_map/ppermute | solution.py:83
  139.1 15.6 %collective-permute-start.24 = (bf16[72,768]{1,0:T(8,128)(2,1)}, bf16[72,768]{1,0:T(8,128)(2,1)}, u32[]{:S(2)}, u32[]{:S(2)}) collective-permute-start(bf16[72,768]{1,0:T(8,128)(2,1)} %get-tuple-element.80), channel_id=1, source_target_pairs={{0,2},{1,3},{2,0},{3,1},{4,6},{5,7},{6,4},{7,5},{8,10},{9,11},{10,... | collective-permute-start | bytes 331784 | tf_op jit(solution)/shard_map/ppermute | solution.py:83
  139.4 15.4 %collective-permute-start.23 = (bf16[72,768]{1,0:T(8,128)(2,1)S(1)}, bf16[72,768]{1,0:T(8,128)(2,1)}, u32[]{:S(2)}, u32[]{:S(2)}) collective-permute-start(bf16[72,768]{1,0:T(8,128)(2,1)S(1)} %get-tuple-element.81), channel_id=1, source_target_pairs={{0,3},{1,0},{2,1},{3,2},{4,7},{5,4},{6,5},{7,6},{8,11},{9,8},{10,9... | collective-permute-start | bytes 331784 | tf_op jit(solution)/shard_map/ppermute | solution.py:83
  156.7 16.2 %collective-permute-start.26 = (bf16[2,136,768]{2,1,0:T(8,128)(2,1)}, bf16[2,136,768]{2,1,0:T(8,128)(2,1)}, u32[]{:S(2)}, u32[]{:S(2)}) collective-permute-start(bf16[2,136,768]{2,1,0:T(8,128)(2,1)} %constant_dynamic-slice_fusion), channel_id=1, source_target_pairs={{0,16},{16,0},{1,17},{17,1},{2,18},{18,2},{3,19},{19,3},{4,20},{20... | collective-permute-start | bytes 1253384 | tf_op jit(solution)/shard_map/ppermute | solution.py:18
  174.6 7.9 %collective-permute-start.29 = (bf16[72,768]{1,0:T(8,128)(2,1)S(1)}, bf16[72,768]{1,0:T(8,128)(2,1)S(1)}, u32[]{:S(2)}, u32[]{:S(2)}) collective-permute-start(bf16[72,768]{1,0:T(8,128)(2,1)S(1)} %get-tuple-element.75), channel_id=1, source_target_pairs={{0,1},{1,2},{2,3},{3,0},{4,5},{5,6},{6,7},{7,4},{8,9},{9,10},{10,1... | collective-permute-start | bytes 331784 | tf_op jit(solution)/shard_map/ppermute | solution.py:83
  174.7 11.2 %collective-permute-start.28 = (bf16[72,768]{1,0:T(8,128)(2,1)S(1)}, bf16[72,768]{1,0:T(8,128)(2,1)S(1)}, u32[]{:S(2)}, u32[]{:S(2)}) collective-permute-start(bf16[72,768]{1,0:T(8,128)(2,1)S(1)} %get-tuple-element.76), channel_id=1, source_target_pairs={{0,2},{1,3},{2,0},{3,1},{4,6},{5,7},{6,4},{7,5},{8,10},{9,11},{10,... | collective-permute-start | bytes 331784 | tf_op jit(solution)/shard_map/ppermute | solution.py:83
  177.1 8.8 %collective-permute-start.27 = (bf16[72,768]{1,0:T(8,128)(2,1)S(1)}, bf16[72,768]{1,0:T(8,128)(2,1)S(1)}, u32[]{:S(2)}, u32[]{:S(2)}) collective-permute-start(bf16[72,768]{1,0:T(8,128)(2,1)S(1)} %get-tuple-element.77), channel_id=1, source_target_pairs={{0,3},{1,0},{2,1},{3,2},{4,7},{5,4},{6,5},{7,6},{8,11},{9,8},{10,9... | collective-permute-start | bytes 331784 | tf_op jit(solution)/shard_map/ppermute | solution.py:83
  (10 other events, 62.2 us)

commit v4 on v3

--- a/solution.py
+++ b/solution.py
@@ -169,11 +169,13 @@
     out_part = jnp.einsum("rhck,rhkd->rcd", by_set(hidden), by_set(w_down), preferred_element_type=F32)
     out_part, late_hidden, grad_share = lax.optimization_barrier((out_part.astype(BF), hidden, grad_share))
     grad_pre_share = (grad_share * silu_slope(pre_share)).astype(BF)
-    grad_pre = share_of_features(grad_pre_share, across(grad_pre_share, pairs), pairs)
+    grad_pre_far = across(grad_pre_share, pairs)
     down_grad = jnp.einsum("pch,pcd->phd", late_hidden, grad_rows, preferred_element_type=F32).astype(BF)
-    grad_pre, down_grad, out_rows = lax.optimization_barrier(
-        (grad_pre, down_grad, sum_over_hidden(out_part))
+    grad_pre_far, down_grad, out_rows = lax.optimization_barrier(
+        (grad_pre_far, down_grad, sum_over_hidden(out_part))
     )
+    grad_pre = share_of_features(grad_pre_share, grad_pre_far, pairs)
+    grad_pre, out_rows = lax.optimization_barrier((grad_pre, out_rows))
     out_home = back_to_tokens(out_rows)
     back_part = jnp.einsum("rhck,rhdk->rcd", by_set(grad_pre), by_set(w_up), preferred_element_type=F32)
     back_part, late_grad_pre, out_home = lax.optimization_barrier(

time: 187 us -> 178 us (0.952)
  waiting for transfers between devices: 44 us -> 34.4 us
    ppermute x18, waiting for transfers between devices: 30.2 us -> 20.7 us  [swap(): return lax.ppermute(value, axis, [(i, i ^ bit) for i in range(count)])]
  transfers between devices with their start and end apart: 30 -> 30, of which waited for: 12 -> 12; matrix products, arithmetic and copies ran while one was open for 47% -> 50% of each run, Pallas kernels for 0% -> 0%
where the time goes in v4:
time: 178 us; the launch traced here: 177 us
  matrix products  84.4 us (47%)
  starting transfers between devices  36 us (20%)
  waiting for transfers between devices  34.4 us (19%)
  other arithmetic  14.5 us (8%)
  local copies, waits for them, and re-layouts  6.78 us (4%)
    ppermute x12, starting transfers between devices, shifted(): lax.ppermute(value, 'expert', [(i, (i + by) % count) for i in range(count)])  21.6 us
    ppermute x18, waiting for transfers between devices, swap(): return lax.ppermute(value, axis, [(i, i ^ bit) for i in range(count)])  20.7 us
    ppermute x18, starting transfers between devices, swap(): return lax.ppermute(value, axis, [(i, i ^ bit) for i in range(count)])  14.4 us
    dot_general x1, matrix products, on_device(): jnp.einsum('pcd,pch->pdh', arrived, late_grad_pre, preferred_element_type...  14.1 us
    dot_general x1, matrix products, on_device(): jnp.einsum('pch,pcd->phd', late_hidden, grad_rows, preferred_element_type...  13.9 us
    ppermute x12, waiting for transfers between devices, shifted(): lax.ppermute(value, 'expert', [(i, (i + by) % count) for i in range(count)])  13.7 us
    dot_general x1, matrix products, on_device(): jnp.einsum('pcd,phd->pch', grad_rows, w_down, preferred_element_type=F32)  13.6 us
    dot_general x1, matrix products, on_device(): jnp.einsum('rhck,rhdk->rcd', by_set(grad_pre), by_set(w_up), preferred_el...  13.2 us
  transfers between devices with their start and end apart: 30, of which 12 were waited for; matrix products, arithmetic and copies ran while one was open for 50% of the time, Pallas kernels for 0%

profile of v4, /device:TPU:0, one launch (start us, length us, event | category | flops | bytes accessed | tf_op | source)
XLA Modules:
  0.0 177.2 jit_solution(11477600033537513958)
XLA Ops:
  2.2 3.1 %collective-permute-start = (bf16[72,768]{1,0:T(8,128)(2,1)S(1)}, bf16[72,768]{1,0:T(8,128)(2,1)S(1)}, u32[]{:S(2)}, u32[]{:S(2)}) collective-permute-start(bf16[72,768]{1,0:T(8,128)(2,1)S(1)} %dynamic-slice_bitcast_fusion.9), channel_id=1, source_target_pairs={{0,1},{1,2},{2,3},{3,0},{4,5},{5,6},{6,7},{7,4},{8,9},{9,10},{10,1... | collective-permute-start | bytes 331784 | tf_op jit(solution)/shard_map/ppermute | solution.py:83
  5.3 2.7 %collective-permute-start.1 = (bf16[72,768]{1,0:T(8,128)(2,1)S(1)}, bf16[72,768]{1,0:T(8,128)(2,1)S(1)}, u32[]{:S(2)}, u32[]{:S(2)}) collective-permute-start(bf16[72,768]{1,0:T(8,128)(2,1)S(1)} %dynamic-slice_bitcast_fusion.8), channel_id=1, source_target_pairs={{0,2},{1,3},{2,0},{3,1},{4,6},{5,7},{6,4},{7,5},{8,10},{9,11},{10,... | collective-permute-start | bytes 331784 | tf_op jit(solution)/shard_map/ppermute | solution.py:83
  7.9 1.4 collective-permute-start.2
  9.7 1.6 collective-permute-done
  11.3 3.9 %collective-permute-done.1 = bf16[72,768]{1,0:T(8,128)(2,1)S(1)} collective-permute-done((bf16[72,768]{1,0:T(8,128)(2,1)S(1)}, bf16[72,768]{1,0:T(8,128)(2,1)S(1)}, u32[]{:S(2)}, u32[]{:S(2)}) %collective-permute-start.1) | collective-permute-done | bytes 110624 | tf_op jit(solution)/shard_map/ppermute | solution.py:83
  15.2 1.5 collective-permute-start.3
  17.3 1.5 collective-permute-start.5
  19.3 2.8 %collective-permute-start.6 = (bf16[72,768]{1,0:T(8,128)(2,1)S(1)}, bf16[72,768]{1,0:T(8,128)(2,1)S(1)}, u32[]{:S(2)}, u32[]{:S(2)}) collective-permute-start(bf16[72,768]{1,0:T(8,128)(2,1)S(1)} %dynamic-slice_bitcast_fusion.6), channel_id=1, source_target_pairs={{0,1},{1,2},{2,3},{3,0},{4,5},{5,6},{6,7},{7,4},{8,9},{9,10},{10,1... | collective-permute-start | bytes 331784 | tf_op jit(solution)/shard_map/ppermute | solution.py:83
  22.2 1.6 collective-permute-start.8
  27.9 11.8 %convolution_convert_fusion.4 = bf16[4,136,2048]{2,1,0:T(8,128)(2,1)S(1)} fusion(bf16[4,136,1536]{2,1,0:T(8,128)(2,1)S(1)} %bitcast.105, bf16[4,1536,2048]{2,1,0:T(8,128)(2,1)} %param.9), kind=kOutput, calls=%fused_computation.4 | convolution fusion | flops 3423666176 | bytes 29065216 | tf_op jit(solution)/shard_map/pcd,pdh->pch/dot_general | solution.py:148
  41.8 2.7 %collective-permute-done.9 = bf16[72,768]{1,0:T(8,128)(2,1)S(1)} collective-permute-done((bf16[72,768]{1,0:T(8,128)(2,1)S(1)}, bf16[72,768]{1,0:T(8,128)(2,1)S(1)}, u32[]{:S(2)}, u32[]{:S(2)}) %collective-permute-start.9) | collective-permute-done | bytes 110624 | tf_op jit(solution)/shard_map/ppermute | solution.py:18
  46.9 2.3 %convolution_convert_fusion.3 = bf16[544,1536]{1,0:T(8,128)(2,1)} fusion(bf16[288,1536]{1,0:T(8,128)(2,1)S(1)} %maximum_maximum_fusion, s32[544]{0:T(1024)S(1)} %fusion.35), kind=kOutput, calls=%fused_computation.3 | convolution fusion | flops 482288640 | bytes 2558080 | tf_op jit(solution)/shard_map/dot_general | solution.py:140
  50.0 1.7 fusion.4
  52.6 1.5 collective-permute-start.13
  54.1 13.6 %convolution_convert_fusion.2 = bf16[4,136,2048]{2,1,0:T(8,128)(2,1)S(1)} fusion(bf16[4,136,1536]{2,1,0:T(8,128)(2,1)} %bitcast.111, bf16[4,2048,1536]{2,1,0:T(8,128)(2,1)} %param.10), kind=kOutput, calls=%fused_computation.2 | convolution fusion | flops 3423666176 | bytes 29065216 | tf_op jit(solution)/shard_map/pcd,phd->pch/dot_general | solution.py:152
  67.8 2.5 %multiply_convert_fusion.1 = (bf16[1,136,2048]{2,1,0:T(8,128)(2,1)S(1)}, f32[1,136,2048]{2,1,0:T(8,128)}) fusion(bf16[1,136,2048]{2,1,0:T(8,128)(2,1)} %collective-permute-done.13, bf16[2,1,136,2048]{3,2,1,0:T(8,128)(2,1)} %copy-done.7, s32[]{:T(128)S(6)} %select_n.279), kind=kLoop, calls=%fused_computation.27 | loop fusion | flops 2228224 | bytes 2785284 | tf_op jit(solution)/shard_map/convert_element_type | solution.py:153
  71.8 1.4 collective-permute-done.15
  73.2 1.4 fusion.3
  74.6 11.0 %collective-permute-done.16 = bf16[1,136,2048]{2,1,0:T(8,128)(2,1)} collective-permute-done((bf16[1,136,2048]{2,1,0:T(8,128)(2,1)S(1)}, bf16[1,136,2048]{2,1,0:T(8,128)(2,1)}, u32[]{:S(2)}, u32[]{:S(2)}) %collective-permute-start.16) | collective-permute-done | bytes 557088 | tf_op jit(solution)/shard_map/ppermute | solution.py:18
  87.9 1.4 broadcast_select_fusion.15
  89.6 10.3 %fusion.1 = bf16[2,136,1536]{2,1,0:T(8,128)(2,1)S(1)} fusion(bf16[2,2,136,2048]{3,2,1,0:T(8,128)(2,1)S(1)} %bitcast.108, bf16[2,2,2048,1536]{3,2,1,0:T(8,128)(2,1)} %bitcast.101), kind=kOutput, calls=%fused_computation.11 | convolution fusion | flops 3422969856 | bytes 28229632 | tf_op jit(solution)/shard_map/rhck,rhkd->rcd/dot_general | solution.py:169
  99.9 1.9 %collective-permute-done.18 = bf16[1,136,2048]{2,1,0:T(8,128)(2,1)S(1)} collective-permute-done((bf16[1,136,2048]{2,1,0:T(8,128)(2,1)S(1)}, bf16[1,136,2048]{2,1,0:T(8,128)(2,1)S(1)}, u32[]{:S(2)}, u32[]{:S(2)}) %collective-permute-start.18) | collective-permute-done | bytes 557088 | tf_op jit(solution)/shard_map/ppermute | solution.py:18
  106.3 13.9 %convolution_convert_fusion.1 = bf16[4,2048,1536]{2,1,0:T(8,128)(2,1)} fusion(bf16[4,136,2048]{2,1,0:T(8,128)(2,1)S(1)} %pad_maximum_fusion, bf16[4,136,1536]{2,1,0:T(8,128)(2,1)} %bitcast.112), kind=kOutput, calls=%fused_computation.1 | convolution fusion | flops 3435134976 | bytes 29065216 | tf_op jit(solution)/shard_map/pch,pcd->phd/dot_general | solution.py:173
  121.8 1.7 collective-permute-done.22
  123.5 1.6 broadcast_select_fusion.11
  126.8 2.5 %collective-permute-start.25 = (bf16[72,768]{1,0:T(8,128)(2,1)}, bf16[72,768]{1,0:T(8,128)(2,1)}, u32[]{:S(2)}, u32[]{:S(2)}) collective-permute-start(bf16[72,768]{1,0:T(8,128)(2,1)} %get-tuple-element.83), channel_id=1, source_target_pairs={{0,1},{1,2},{2,3},{3,0},{4,5},{5,6},{6,7},{7,4},{8,9},{9,10},{10,1... | collective-permute-start | bytes 331784 | tf_op jit(solution)/shard_map/ppermute | solution.py:83
  129.6 2.2 %collective-permute-start.23 = (bf16[72,768]{1,0:T(8,128)(2,1)S(1)}, bf16[72,768]{1,0:T(8,128)(2,1)}, u32[]{:S(2)}, u32[]{:S(2)}) collective-permute-start(bf16[72,768]{1,0:T(8,128)(2,1)S(1)} %get-tuple-element.85), channel_id=1, source_target_pairs={{0,3},{1,0},{2,1},{3,2},{4,7},{5,4},{6,5},{7,6},{8,11},{9,8},{10,9... | collective-permute-start | bytes 331784 | tf_op jit(solution)/shard_map/ppermute | solution.py:83
  131.8 13.2 %fusion.2 = bf16[2,136,1536]{2,1,0:T(8,128)(2,1)S(1)} fusion(bf16[2,2,136,2048]{3,2,1,0:T(8,128)(2,1)S(1)} %bitcast.107, bf16[2,2,1536,2048]{3,2,1,0:T(8,128)(2,1)} %bitcast.102), kind=kOutput, calls=%fused_computation.12 | convolution fusion | flops 3422969856 | bytes 28229632 | tf_op jit(solution)/shard_map/rhck,rhdk->rcd/dot_general | solution.py:180
  148.2 14.1 %convolution_convert_fusion = bf16[4,1536,2048]{2,1,0:T(8,128)(2,1)} fusion(bf16[4,136,1536]{2,1,0:T(8,128)(2,1)S(1)} %bitcast.106, bf16[4,136,2048]{2,1,0:T(8,128)(2,1)} %copy-done.4), kind=kOutput, calls=%fused_computation | convolution fusion | flops 3435134976 | bytes 29065216 | tf_op jit(solution)/shard_map/pcd,pch->pdh/dot_general | solution.py:184
  165.2 2.6 %collective-permute-start.28 = (bf16[72,768]{1,0:T(8,128)(2,1)S(1)}, bf16[72,768]{1,0:T(8,128)(2,1)S(1)}, u32[]{:S(2)}, u32[]{:S(2)}) collective-permute-start(bf16[72,768]{1,0:T(8,128)(2,1)S(1)} %get-tuple-element.80), channel_id=1, source_target_pairs={{0,2},{1,3},{2,0},{3,1},{4,6},{5,7},{6,4},{7,5},{8,10},{9,11},{10,... | collective-permute-start | bytes 331784 | tf_op jit(solution)/shard_map/ppermute | solution.py:83
  169.0 4.0 %collective-permute-done.29 = bf16[72,768]{1,0:T(8,128)(2,1)S(1)} collective-permute-done((bf16[72,768]{1,0:T(8,128)(2,1)S(1)}, bf16[72,768]{1,0:T(8,128)(2,1)S(1)}, u32[]{:S(2)}, u32[]{:S(2)}) %collective-permute-start.29) | collective-permute-done | bytes 110624 | tf_op jit(solution)/shard_map/ppermute | solution.py:83
  173.0 3.2 %collective-permute-done.28 = bf16[72,768]{1,0:T(8,128)(2,1)S(1)} collective-permute-done((bf16[72,768]{1,0:T(8,128)(2,1)S(1)}, bf16[72,768]{1,0:T(8,128)(2,1)S(1)}, u32[]{:S(2)}, u32[]{:S(2)}) %collective-permute-start.28) | collective-permute-done | bytes 110624 | tf_op jit(solution)/shard_map/ppermute | solution.py:83
  (113 shorter events, 33.5 us)
Async XLA Ops:
  1.7 17.1 %copy-start.8 = (bf16[128,1536]{1,0:T(8,128)(2,1)S(1)}, bf16[128,1536]{1,0:T(8,128)(2,1)}, u32[]{:S(2)}) copy-start(bf16[128,1536]{1,0:T(8,128)(2,1)} %param.11) | copy-start | bytes 1179652
  2.2 9.1 %collective-permute-start = (bf16[72,768]{1,0:T(8,128)(2,1)S(1)}, bf16[72,768]{1,0:T(8,128)(2,1)S(1)}, u32[]{:S(2)}, u32[]{:S(2)}) collective-permute-start(bf16[72,768]{1,0:T(8,128)(2,1)S(1)} %dynamic-slice_bitcast_fusion.9), channel_id=1, source_target_pairs={{0,1},{1,2},{2,3},{3,0},{4,5},{5,6},{6,7},{7,4},{8,9},{9,10},{10,1... | collective-permute-start | bytes 331784 | tf_op jit(solution)/shard_map/ppermute | solution.py:83
  5.3 9.9 %collective-permute-start.1 = (bf16[72,768]{1,0:T(8,128)(2,1)S(1)}, bf16[72,768]{1,0:T(8,128)(2,1)S(1)}, u32[]{:S(2)}, u32[]{:S(2)}) collective-permute-start(bf16[72,768]{1,0:T(8,128)(2,1)S(1)} %dynamic-slice_bitcast_fusion.8), channel_id=1, source_target_pairs={{0,2},{1,3},{2,0},{3,1},{4,6},{5,7},{6,4},{7,5},{8,10},{9,11},{10,... | collective-permute-start | bytes 331784 | tf_op jit(solution)/shard_map/ppermute | solution.py:83
  7.9 7.3 %collective-permute-start.2 = (bf16[72,768]{1,0:T(8,128)(2,1)S(1)}, bf16[72,768]{1,0:T(8,128)(2,1)S(1)}, u32[]{:S(2)}, u32[]{:S(2)}) collective-permute-start(bf16[72,768]{1,0:T(8,128)(2,1)S(1)} %dynamic-slice_bitcast_fusion.7), channel_id=1, source_target_pairs={{0,3},{1,0},{2,1},{3,2},{4,7},{5,4},{6,5},{7,6},{8,11},{9,8},{10,9... | collective-permute-start | bytes 331784 | tf_op jit(solution)/shard_map/ppermute | solution.py:83
  15.2 8.5 %collective-permute-start.3 = (bf16[72,768]{1,0:T(8,128)(2,1)S(1)}, bf16[72,768]{1,0:T(8,128)(2,1)S(1)}, u32[]{:S(2)}, u32[]{:S(2)}) collective-permute-start(bf16[72,768]{1,0:T(8,128)(2,1)S(1)} %collective-permute-done), channel_id=1, source_target_pairs={{0,16},{16,0},{1,17},{17,1},{2,18},{18,2},{3,19},{19,3},{4,20},{20... | collective-permute-start | bytes 331784 | tf_op jit(solution)/shard_map/ppermute | solution.py:18
  16.8 8.2 %collective-permute-start.4 = (bf16[72,768]{1,0:T(8,128)(2,1)S(1)}, bf16[72,768]{1,0:T(8,128)(2,1)S(1)}, u32[]{:S(2)}, u32[]{:S(2)}) collective-permute-start(bf16[72,768]{1,0:T(8,128)(2,1)S(1)} %collective-permute-done.1), channel_id=1, source_target_pairs={{0,16},{16,0},{1,17},{17,1},{2,18},{18,2},{3,19},{19,3},{4,20},{20... | collective-permute-start | bytes 331784 | tf_op jit(solution)/shard_map/ppermute | solution.py:18
  17.3 7.8 %collective-permute-start.5 = (bf16[72,768]{1,0:T(8,128)(2,1)S(1)}, bf16[72,768]{1,0:T(8,128)(2,1)S(1)}, u32[]{:S(2)}, u32[]{:S(2)}) collective-permute-start(bf16[72,768]{1,0:T(8,128)(2,1)S(1)} %collective-permute-done.2), channel_id=1, source_target_pairs={{0,16},{16,0},{1,17},{17,1},{2,18},{18,2},{3,19},{19,3},{4,20},{20... | collective-permute-start | bytes 331784 | tf_op jit(solution)/shard_map/ppermute | solution.py:18
  19.3 7.7 %collective-permute-start.6 = (bf16[72,768]{1,0:T(8,128)(2,1)S(1)}, bf16[72,768]{1,0:T(8,128)(2,1)S(1)}, u32[]{:S(2)}, u32[]{:S(2)}) collective-permute-start(bf16[72,768]{1,0:T(8,128)(2,1)S(1)} %dynamic-slice_bitcast_fusion.6), channel_id=1, source_target_pairs={{0,1},{1,2},{2,3},{3,0},{4,5},{5,6},{6,7},{7,4},{8,9},{9,10},{10,1... | collective-permute-start | bytes 331784 | tf_op jit(solution)/shard_map/ppermute | solution.py:83
  22.2 17.5 %collective-permute-start.8 = (bf16[72,768]{1,0:T(8,128)(2,1)S(1)}, bf16[72,768]{1,0:T(8,128)(2,1)S(1)}, u32[]{:S(2)}, u32[]{:S(2)}) collective-permute-start(bf16[72,768]{1,0:T(8,128)(2,1)S(1)} %dynamic-slice_bitcast_fusion.5), channel_id=1, source_target_pairs={{0,2},{1,3},{2,0},{3,1},{4,6},{5,7},{6,4},{7,5},{8,10},{9,11},{10,... | collective-permute-start | bytes 331784 | tf_op jit(solution)/shard_map/ppermute | solution.py:83
  23.8 17.2 %collective-permute-start.10 = (bf16[72,768]{1,0:T(8,128)(2,1)S(1)}, bf16[72,768]{1,0:T(8,128)(2,1)S(1)}, u32[]{:S(2)}, u32[]{:S(2)}) collective-permute-start(bf16[72,768]{1,0:T(8,128)(2,1)S(1)} %dynamic-slice_bitcast_fusion.4), channel_id=1, source_target_pairs={{0,3},{1,0},{2,1},{3,2},{4,7},{5,4},{6,5},{7,6},{8,11},{9,8},{10,9... | collective-permute-start | bytes 331784 | tf_op jit(solution)/shard_map/ppermute | solution.py:83
  26.2 13.5 %copy-start.2 = (bf16[544,1536]{1,0:T(8,128)(2,1)}, bf16[544,1536]{1,0:T(8,128)(2,1)S(1)}, u32[]{:S(2)}) copy-start(bf16[544,1536]{1,0:T(8,128)(2,1)S(1)} %convolution_convert_fusion.5) | copy-start | bytes 5013508
  27.1 14.7 %collective-permute-start.7 = (bf16[72,768]{1,0:T(8,128)(2,1)S(1)}, bf16[72,768]{1,0:T(8,128)(2,1)S(1)}, u32[]{:S(2)}, u32[]{:S(2)}) collective-permute-start(bf16[72,768]{1,0:T(8,128)(2,1)S(1)} %collective-permute-done.6), channel_id=1, source_target_pairs={{0,16},{16,0},{1,17},{17,1},{2,18},{18,2},{3,19},{19,3},{4,20},{20... | collective-permute-start | bytes 331784 | tf_op jit(solution)/shard_map/ppermute | solution.py:18
  39.7 4.8 %collective-permute-start.9 = (bf16[72,768]{1,0:T(8,128)(2,1)S(1)}, bf16[72,768]{1,0:T(8,128)(2,1)S(1)}, u32[]{:S(2)}, u32[]{:S(2)}) collective-permute-start(bf16[72,768]{1,0:T(8,128)(2,1)S(1)} %collective-permute-done.8), channel_id=1, source_target_pairs={{0,16},{16,0},{1,17},{17,1},{2,18},{18,2},{3,19},{19,3},{4,20},{20... | collective-permute-start | bytes 331784 | tf_op jit(solution)/shard_map/ppermute | solution.py:18
  41.0 4.7 %collective-permute-start.11 = (bf16[72,768]{1,0:T(8,128)(2,1)S(1)}, bf16[72,768]{1,0:T(8,128)(2,1)S(1)}, u32[]{:S(2)}, u32[]{:S(2)}) collective-permute-start(bf16[72,768]{1,0:T(8,128)(2,1)S(1)} %collective-permute-done.10), channel_id=1, source_target_pairs={{0,16},{16,0},{1,17},{17,1},{2,18},{18,2},{3,19},{19,3},{4,20},{20... | collective-permute-start | bytes 331784 | tf_op jit(solution)/shard_map/ppermute | solution.py:18
  46.9 3.1 %collective-permute-start.12 = (bf16[2,1,136,2048]{3,2,1,0:T(8,128)(2,1)}, bf16[2,1,136,2048]{3,2,1,0:T(8,128)(2,1)}, u32[]{:S(2)}, u32[]{:S(2)}) collective-permute-start(bf16[2,1,136,2048]{3,2,1,0:T(8,128)(2,1)} %dynamic-slice_bitcast_fusion.1), channel_id=1, source_target_pairs={{0,4},{4,0},{8,12},{12,8},{1,5},{5,1},{9,13},{13,9},{2,6},{6,2},{1... | collective-permute-start | bytes 3342344 | tf_op jit(solution)/shard_map/ppermute | solution.py:18
  52.6 15.1 %collective-permute-start.13 = (bf16[1,136,2048]{2,1,0:T(8,128)(2,1)S(1)}, bf16[1,136,2048]{2,1,0:T(8,128)(2,1)}, u32[]{:S(2)}, u32[]{:S(2)}) collective-permute-start(bf16[1,136,2048]{2,1,0:T(8,128)(2,1)S(1)} %dynamic-slice_bitcast_fusion.3), channel_id=1, source_target_pairs={{0,8},{4,12},{8,0},{12,4},{1,9},{5,13},{9,1},{13,5},{2,10},{6,14},... | collective-permute-start | bytes 1671176 | tf_op jit(solution)/shard_map/ppermute | solution.py:18
  70.4 2.8 %collective-permute-start.15 = (bf16[2,1,136,2048]{3,2,1,0:T(8,128)(2,1)S(1)}, bf16[2,1,136,2048]{3,2,1,0:T(8,128)(2,1)S(1)}, u32[]{:S(2)}, u32[]{:S(2)}) collective-permute-start(bf16[2,1,136,2048]{3,2,1,0:T(8,128)(2,1)S(1)} %dynamic-slice_bitcast_fusion), channel_id=1, source_target_pairs={{0,4},{4,0},{8,12},{12,8},{1,5},{5,1},{9,13},{13,9},{2,6},{6,2},{1... | collective-permute-start | bytes 3342344 | tf_op jit(solution)/shard_map/ppermute | solution.py:18
  70.5 15.1 %collective-permute-start.16 = (bf16[1,136,2048]{2,1,0:T(8,128)(2,1)S(1)}, bf16[1,136,2048]{2,1,0:T(8,128)(2,1)}, u32[]{:S(2)}, u32[]{:S(2)}) collective-permute-start(bf16[1,136,2048]{2,1,0:T(8,128)(2,1)S(1)} %get-tuple-element.39), channel_id=1, source_target_pairs={{0,8},{4,12},{8,0},{12,4},{1,9},{5,13},{9,1},{13,5},{2,10},{6,14},... | collective-permute-start | bytes 1671176 | tf_op jit(solution)/shard_map/ppermute | solution.py:18
  71.7 16.2 %collective-permute-start.14 = (bf16[1,136,2048]{2,1,0:T(8,128)(2,1)S(1)}, bf16[1,136,2048]{2,1,0:T(8,128)(2,1)}, u32[]{:S(2)}, u32[]{:S(2)}) collective-permute-start(bf16[1,136,2048]{2,1,0:T(8,128)(2,1)S(1)} %get-tuple-element.39), channel_id=1, source_target_pairs={{0,4},{4,0},{8,12},{12,8},{1,5},{5,1},{9,13},{13,9},{2,6},{6,2},{1... | collective-permute-start | bytes 1671176 | tf_op jit(solution)/shard_map/ppermute | solution.py:18
  85.6 2.3 %collective-permute-start.17 = (bf16[1,136,2048]{2,1,0:T(8,128)(2,1)}, bf16[1,136,2048]{2,1,0:T(8,128)(2,1)S(1)}, u32[]{:S(2)}, u32[]{:S(2)}) collective-permute-start(bf16[1,136,2048]{2,1,0:T(8,128)(2,1)} %collective-permute-done.16), channel_id=1, source_target_pairs={{0,4},{4,0},{8,12},{12,8},{1,5},{5,1},{9,13},{13,9},{2,6},{6,2},{1... | collective-permute-start | bytes 1671176 | tf_op jit(solution)/shard_map/ppermute | solution.py:18
  86.7 15.1 %collective-permute-start.18 = (bf16[1,136,2048]{2,1,0:T(8,128)(2,1)S(1)}, bf16[1,136,2048]{2,1,0:T(8,128)(2,1)S(1)}, u32[]{:S(2)}, u32[]{:S(2)}) collective-permute-start(bf16[1,136,2048]{2,1,0:T(8,128)(2,1)S(1)} %dynamic-slice_bitcast_fusion.2), channel_id=1, source_target_pairs={{0,8},{4,12},{8,0},{12,4},{1,9},{5,13},{9,1},{13,5},{2,10},{6,14},... | collective-permute-start | bytes 1671176 | tf_op jit(solution)/shard_map/ppermute | solution.py:18
  103.2 18.1 %collective-permute-start.20 = (bf16[1,136,2048]{2,1,0:T(8,128)(2,1)}, bf16[1,136,2048]{2,1,0:T(8,128)(2,1)}, u32[]{:S(2)}, u32[]{:S(2)}) collective-permute-start(bf16[1,136,2048]{2,1,0:T(8,128)(2,1)} %multiply_convert_fusion), channel_id=1, source_target_pairs={{0,8},{4,12},{8,0},{12,4},{1,9},{5,13},{9,1},{13,5},{2,10},{6,14},... | collective-permute-start | bytes 1671176 | tf_op jit(solution)/shard_map/ppermute | solution.py:18
  104.3 17.5 %collective-permute-start.19 = (bf16[1,136,2048]{2,1,0:T(8,128)(2,1)}, bf16[1,136,2048]{2,1,0:T(8,128)(2,1)}, u32[]{:S(2)}, u32[]{:S(2)}) collective-permute-start(bf16[1,136,2048]{2,1,0:T(8,128)(2,1)} %multiply_convert_fusion), channel_id=1, source_target_pairs={{0,4},{4,0},{8,12},{12,8},{1,5},{5,1},{9,13},{13,9},{2,6},{6,2},{1... | collective-permute-start | bytes 1671176 | tf_op jit(solution)/shard_map/ppermute | solution.py:18
  105.1 15.1 %collective-permute-start.21 = (bf16[2,136,768]{2,1,0:T(8,128)(2,1)}, bf16[2,136,768]{2,1,0:T(8,128)(2,1)}, u32[]{:S(2)}, u32[]{:S(2)}) collective-permute-start(bf16[2,136,768]{2,1,0:T(8,128)(2,1)} %constant_dynamic-slice_fusion.1), channel_id=1, source_target_pairs={{0,16},{16,0},{1,17},{17,1},{2,18},{18,2},{3,19},{19,3},{4,20},{20... | collective-permute-start | bytes 1253384 | tf_op jit(solution)/shard_map/ppermute | solution.py:18
  121.3 2.2 %collective-permute-start.22 = (bf16[1,136,2048]{2,1,0:T(8,128)(2,1)}, bf16[1,136,2048]{2,1,0:T(8,128)(2,1)S(1)}, u32[]{:S(2)}, u32[]{:S(2)}) collective-permute-start(bf16[1,136,2048]{2,1,0:T(8,128)(2,1)} %collective-permute-done.20), channel_id=1, source_target_pairs={{0,4},{4,0},{8,12},{12,8},{1,5},{5,1},{9,13},{13,9},{2,6},{6,2},{1... | collective-permute-start | bytes 1671176 | tf_op jit(solution)/shard_map/ppermute | solution.py:18
  126.8 18.3 %collective-permute-start.25 = (bf16[72,768]{1,0:T(8,128)(2,1)}, bf16[72,768]{1,0:T(8,128)(2,1)}, u32[]{:S(2)}, u32[]{:S(2)}) collective-permute-start(bf16[72,768]{1,0:T(8,128)(2,1)} %get-tuple-element.83), channel_id=1, source_target_pairs={{0,1},{1,2},{2,3},{3,0},{4,5},{5,6},{6,7},{7,4},{8,9},{9,10},{10,1... | collective-permute-start | bytes 331784 | tf_op jit(solution)/shard_map/ppermute | solution.py:83
  129.3 15.8 %collective-permute-start.24 = (bf16[72,768]{1,0:T(8,128)(2,1)}, bf16[72,768]{1,0:T(8,128)(2,1)}, u32[]{:S(2)}, u32[]{:S(2)}) collective-permute-start(bf16[72,768]{1,0:T(8,128)(2,1)} %get-tuple-element.84), channel_id=1, source_target_pairs={{0,2},{1,3},{2,0},{3,1},{4,6},{5,7},{6,4},{7,5},{8,10},{9,11},{10,... | collective-permute-start | bytes 331784 | tf_op jit(solution)/shard_map/ppermute | solution.py:83
  129.6 15.5 %collective-permute-start.23 = (bf16[72,768]{1,0:T(8,128)(2,1)S(1)}, bf16[72,768]{1,0:T(8,128)(2,1)}, u32[]{:S(2)}, u32[]{:S(2)}) collective-permute-start(bf16[72,768]{1,0:T(8,128)(2,1)S(1)} %get-tuple-element.85), channel_id=1, source_target_pairs={{0,3},{1,0},{2,1},{3,2},{4,7},{5,4},{6,5},{7,6},{8,11},{9,8},{10,9... | collective-permute-start | bytes 331784 | tf_op jit(solution)/shard_map/ppermute | solution.py:83
  147.1 16.4 %collective-permute-start.26 = (bf16[2,136,768]{2,1,0:T(8,128)(2,1)}, bf16[2,136,768]{2,1,0:T(8,128)(2,1)}, u32[]{:S(2)}, u32[]{:S(2)}) collective-permute-start(bf16[2,136,768]{2,1,0:T(8,128)(2,1)} %constant_dynamic-slice_fusion), channel_id=1, source_target_pairs={{0,16},{16,0},{1,17},{17,1},{2,18},{18,2},{3,19},{19,3},{4,20},{20... | collective-permute-start | bytes 1253384 | tf_op jit(solution)/shard_map/ppermute | solution.py:18
  165.1 7.9 %collective-permute-start.29 = (bf16[72,768]{1,0:T(8,128)(2,1)S(1)}, bf16[72,768]{1,0:T(8,128)(2,1)S(1)}, u32[]{:S(2)}, u32[]{:S(2)}) collective-permute-start(bf16[72,768]{1,0:T(8,128)(2,1)S(1)} %get-tuple-element.79), channel_id=1, source_target_pairs={{0,1},{1,2},{2,3},{3,0},{4,5},{5,6},{6,7},{7,4},{8,9},{9,10},{10,1... | collective-permute-start | bytes 331784 | tf_op jit(solution)/shard_map/ppermute | solution.py:83
  165.2 11.0 %collective-permute-start.28 = (bf16[72,768]{1,0:T(8,128)(2,1)S(1)}, bf16[72,768]{1,0:T(8,128)(2,1)S(1)}, u32[]{:S(2)}, u32[]{:S(2)}) collective-permute-start(bf16[72,768]{1,0:T(8,128)(2,1)S(1)} %get-tuple-element.80), channel_id=1, source_target_pairs={{0,2},{1,3},{2,0},{3,1},{4,6},{5,7},{6,4},{7,5},{8,10},{9,11},{10,... | collective-permute-start | bytes 331784 | tf_op jit(solution)/shard_map/ppermute | solution.py:83
  167.8 8.5 %collective-permute-start.27 = (bf16[72,768]{1,0:T(8,128)(2,1)S(1)}, bf16[72,768]{1,0:T(8,128)(2,1)S(1)}, u32[]{:S(2)}, u32[]{:S(2)}) collective-permute-start(bf16[72,768]{1,0:T(8,128)(2,1)S(1)} %get-tuple-element.81), channel_id=1, source_target_pairs={{0,3},{1,0},{2,1},{3,2},{4,7},{5,4},{6,5},{7,6},{8,11},{9,8},{10,9... | collective-permute-start | bytes 331784 | tf_op jit(solution)/shard_map/ppermute | solution.py:83
  (10 other events, 52.1 us)
